TPU v7x, 512 devices: a whole 4x4x16 slice. The times are simulated.
512 devices in a mesh: owner: 64 (over y, z), grp: 8 (over x, core).
Axes of the slice: x: 4, y: 4, z: 16, core: 2. Of those that a mesh axis runs over, the one named last changes fastest.
Arguments:
- sources: bfloat16 [16, 524288], P(None, ('owner', 'grp')), may hold values from -6 to 6
- near_pairs: int32 [8192, 2], P(('owner', 'grp')), may hold values from 0 to 2047, as said below
- near_blocks: bfloat16 [8192, 256, 256], P(('owner', 'grp')), may hold values from -0.375 to 0.375
- far_pairs: int32 [32768, 2], P(('owner', 'grp')), may hold values from 0 to 2047, as said below
- far_left: bfloat16 [32768, 32, 256], P(('owner', 'grp')), may hold values from -1 to 1
- far_right: bfloat16 [32768, 32, 256], P(('owner', 'grp')), may hold values from -0.375 to 0.375
Outputs:
- potential: bfloat16 [16, 524288], P(None, ('owner', 'grp'))
Inputs may be any that keep to these rules, and one draw needn't show every extreme that they name: `near_pairs`: each row is (target, source); the target is a cluster held by the device that holds the row, and the source a cluster held by a device with the same owner index. `far_pairs`: each row is (target, source); the target is a cluster held by the device that holds the row, and the source a cluster held by a device with the same grp index. The rows of one device name sources on one owner index at most 2 times, and exactly 2 times for some owner index.
All inputs are finite; a program needn't handle non-finite values.
Results may differ from a plain program's by a relative error of at most 0.0085.
Values may be sent and summed in bfloat16 or wider, within the bound.
No kernel may reach another device: no remote copies, remote signals or barrier semaphores. Data moves between devices by JAX's collectives and lax.ppermute only.
A program may use at most 64 MiB of HBM per device.

v0:
```python
import jax
import jax.numpy as jnp
from jax import lax
from jax.sharding import PartitionSpec as P

P_SIZE = 256
CAP = 2
CL = 4


def add_rows(values, targets, count):
    onehot = (targets[:, None] == jnp.arange(count)[None, :]).astype(jnp.float32)
    return jnp.einsum("rnp,nc->rcp", values, onehot, precision=lax.Precision.HIGHEST)


def on_device(sources, near_pairs, near_blocks, far_pairs, far_left, far_right):
    rhs = sources.shape[0]
    n_owner = lax.axis_size("owner")
    n_group = lax.axis_size("grp")
    region = lax.axis_index("owner")
    device = region * n_group + lax.axis_index("grp")
    local = sources.reshape(rhs, CL, P_SIZE)
    grouped = lax.all_gather(sources, "grp", axis=1, tiled=True).reshape(rhs, n_group * CL, P_SIZE)
    near_target = near_pairs[:, 0] - device * CL
    near_source = near_pairs[:, 1] - region * n_group * CL
    source_blocks = jnp.take(grouped, near_source, axis=1)
    target_blocks = jnp.take(local, near_target, axis=1)
    forward = jnp.einsum(
        "rnq,npq->rnp", source_blocks, near_blocks, preferred_element_type=jnp.float32
    )
    backward = jnp.einsum(
        "rnp,npq->rnq", target_blocks, near_blocks, preferred_element_type=jnp.float32
    )
    total = add_rows(forward, near_target, CL)
    spread = add_rows(backward, near_source, n_group * CL).reshape(rhs, n_group * CL * P_SIZE)
    total = total + lax.psum_scatter(
        spread.astype(jnp.bfloat16), "grp", scatter_dimension=1, tiled=True
    ).astype(jnp.float32).reshape(rhs, CL, P_SIZE)
    far_target = far_pairs[:, 0] - device * CL
    far_source = far_pairs[:, 1]
    peer = far_source // CL // n_group
    within = far_source % CL
    slot_count = n_owner * CAP
    peer_hot = (peer[:, None] == jnp.arange(n_owner)[None, :]).astype(jnp.int32)
    order = jnp.sum(jnp.cumsum(peer_hot, axis=0) * peer_hot, axis=1) - 1
    slot = peer * CAP + order
    wanted = jnp.zeros((slot_count,), jnp.int32).at[slot].set(within)
    asked = lax.all_to_all(
        wanted.reshape(n_owner, CAP), "owner", split_axis=0, concat_axis=0, tiled=True
    ).reshape(slot_count)
    everyone = lax.all_gather(sources, "owner", axis=1, tiled=True).reshape(
        rhs, n_owner * CL, P_SIZE
    )
    far_blocks = jnp.take(everyone, peer * CL + within, axis=1)
    coef = jnp.einsum(
        "rnq,nkq->rnk", far_blocks, far_right, preferred_element_type=jnp.float32
    ).astype(jnp.bfloat16)
    far_forward = jnp.einsum("rnk,nkp->rnp", coef, far_left, preferred_element_type=jnp.float32)
    total = total + add_rows(far_forward, far_target, CL)
    target_far = jnp.take(local, far_target, axis=1)
    coef_back = jnp.einsum(
        "rnp,nkp->rnk", target_far, far_left, preferred_element_type=jnp.float32
    ).astype(jnp.bfloat16)
    far_backward = jnp.einsum(
        "rnk,nkq->rnq", coef_back, far_right, preferred_element_type=jnp.float32
    )
    outgoing = jnp.zeros((rhs, slot_count, P_SIZE), jnp.float32).at[:, slot].set(far_backward)
    incoming = lax.all_to_all(
        outgoing.reshape(rhs, n_owner, CAP, P_SIZE),
        "owner",
        split_axis=1,
        concat_axis=1,
        tiled=True,
    ).reshape(rhs, slot_count, P_SIZE)
    total = total + add_rows(incoming, asked, CL)
    return total.reshape(rhs, CL * P_SIZE).astype(jnp.bfloat16)


def solution(mesh):
    placed = (
        P(None, ("owner", "grp")),
        P(("owner", "grp"), None),
        P(("owner", "grp"), None, None),
        P(("owner", "grp"), None),
        P(("owner", "grp"), None, None),
        P(("owner", "grp"), None, None),
    )
    return jax.shard_map(
        on_device, mesh=mesh, in_specs=placed, out_specs=P(None, ("owner", "grp")), check_vma=False
    )
```

profile of v0, /device:TPU:4, one launch (start us, length us, event | category | flops | bytes accessed | tf_op | source)
XLA Modules:
  0.0 257.6 jit_solution(986273858305495811)
XLA Ops:
  7.4 0.0 copy-start
  7.4 0.8 and_select_fusion
  8.2 0.8 fusion.60
  9.0 0.8 and_bitcast_fusion.1
  9.7 0.1 fusion.34
  9.8 0.1 reduce_window_sum.11
  9.9 0.2 select_reduce_fusion
  10.1 0.8 scatter_custom_fusion
  10.9 0.8 all_to_all.9
  11.7 18.7 %all-to-all-start = ((s32[64,1,2]{2,1,0:T(1,128)}), s32[64,1,2]{2,1,0:T(1,128)S(1)}, u32[]{:S(2)}, u32[]{:S(2)}) async-start(s32[64,1,2]{2,1,0:T(1,128)} %bitcast.26), calls=%async_computation.1 | async-start | bytes 65536 | tf_op jit(solution)/shard_map/all_to_all | solution.py:48
  30.4 0.8 copy.43
  31.2 1.4 gather_fusion.3
  32.5 2.3 fusion.2
  34.8 1.6 broadcast_in_dim.59
  36.4 8.1 %scatter_fusion = f32[16,128,256]{2,0,1:T(8,128)} fusion(f32[16,128,256]{2,0,1:T(8,128)} %broadcast_in_dim.59, s32[64]{0:T(128)S(1)} %fusion.49, f32[64,16,256]{2,1,0:T(8,128)S(1)} %fusion.2), kind=kCustom, calls=%fused_computation.5 | custom fusion | bytes 3145984 | tf_op jit(solution)/shard_map/scatter | solution.py:67
  44.6 4.8 %copy.25 = f32[16,64,2,256]{3,2,0,1:T(2,128)} copy(f32[16,64,2,256]{3,0,2,1:T(8,128)} %bitcast.112) | data formatting | bytes 4194304 | tf_op jit(solution)/shard_map/reshape | solution.py:69
  49.4 0.0 copy-start.2
  49.4 0.0 all-to-all-done
  49.4 15.5 %all-to-all-start.1 = ((f32[16,64,2,256]{3,2,0,1:T(2,128)}), f32[16,64,2,256]{3,2,0,1:T(2,128)}, u32[]{:S(2)}, u32[]{:S(2)}) async-start(f32[16,64,2,256]{3,2,0,1:T(2,128)} %copy.25), calls=%async_computation.2 | async-start | bytes 4194304 | tf_op jit(solution)/shard_map/all_to_all | solution.py:68
  64.9 0.0 copy-start.1
  64.9 0.0 reduce-scatter.2.cloned.1.call-start
  65.0 0.0 copy-done.2
  65.0 0.6 gather_fusion.1
  65.6 0.0 copy-done
  65.6 0.4 convolution_bitcast_fusion.1
  66.0 0.6 convolution_convert_fusion.2
  66.6 0.9 copy.30
  67.5 0.0 reduce-scatter.2.cloned.1.call-update
  67.5 0.0 all-gather.2.cloned.1.call-start
  67.5 0.5 all-gather.2.cloned.1.call-update
  68.1 0.0 copy-done.1
  68.1 11.8 %all_gather.6 = bf16[16,8192]{1,0:T(8,128)(2,1)S(1)} all-gather(bf16[16,1024]{1,0:T(8,128)(2,1)S(1)} %copy-done.1), channel_id=1, replica_groups=mesh['owner'=64,'grp'=8] {'grp'}, dimensions={1}, use_global_device_ids=true | all-gather | bytes 294912 | tf_op jit(solution)/shard_map/all_gather | solution.py:23
  79.9 0.6 gather_fusion
  80.5 0.7 convolution_bitcast_fusion.2
  81.2 0.5 broadcast.259
  81.7 0.7 reduce.3
  82.4 0.1 eq.93
  82.6 20.5 %reduce-scatter.2.cloned.1.call-done = bf16[16,1024]{1,0:T(8,128)(2,1)} async-done(((bf16[16,8192]{1,0:T(8,128)(2,1)}), bf16[16,1024]{1,0:T(8,128)(2,1)}) %reduce-scatter.2.cloned.1.call-update) | async-done | bytes 32784 | tf_op jit(solution)/shard_map/reduce_scatter | solution.py:36
  103.0 0.8 reshape.64
  103.8 0.4 fusion.5
  104.2 125.8 %all-gather.2.cloned.1.call-done = bf16[16,65536]{1,0:T(8,128)(2,1)} async-done(((bf16[16,1024]{1,0:T(8,128)(2,1)}), bf16[16,65536]{1,0:T(8,128)(2,1)}) %all-gather.2.cloned.1.call-update) | async-done | bytes 2097168 | tf_op jit(solution)/shard_map/all_gather | solution.py:51
  230.0 3.1 %copy.41 = bf16[2,256,8,256]{3,2,0,1:T(8,128)(2,1)} copy(bf16[2,256,8,256]{3,2,1,0:T(8,128)(2,1)} %bitcast.114) | data formatting | bytes 4194304 | tf_op jit(solution)/shard_map/reshape | solution.py:51
  233.1 3.0 %gather_fusion.2 = bf16[64,16,256]{2,1,0:T(8,128)(2,1)} fusion(bf16[16,256,256]{2,0,1:T(8,128)(2,1)} %bitcast.113, s32[1024]{0:T(1024)S(1)} %pad_clamp_fusion.1), kind=kCustom, calls=%fused_computation.2 | custom fusion | bytes 1048832 | tf_op jit(solution)/shard_map/jit(_take)/gather | solution.py:54
  236.1 2.3 convolution_bitcast_fusion
  238.4 1.0 fusion.4
  239.4 0.0 all-to-all-done.1
  239.4 4.0 %copy.26 = f32[16,64,2,256]{3,2,1,0:T(2,128)} copy(f32[16,64,2,256]{3,2,0,1:T(2,128)} %all-to-all-done.1) | data formatting | bytes 4194304 | tf_op jit(solution)/shard_map/all_to_all | solution.py:68
  243.4 3.7 %reshape.62 = f32[16,128,256]{2,1,0:T(8,128)} reshape(f32[16,64,2,256]{3,2,1,0:T(2,128)} %copy.26) | data formatting | bytes 4194304 | tf_op jit(solution)/shard_map/reshape | solution.py:74
  247.1 2.4 fusion.6
  249.5 0.6 copy.31
  (8 shorter events, 0.1 us)
Async XLA Ops:
  7.4 58.2 %copy-start = (bf16[16,256,256]{2,1,0:T(8,128)(2,1)S(1)}, bf16[16,256,256]{2,1,0:T(8,128)(2,1)}, u32[]{:S(2)}) copy-start(bf16[16,256,256]{2,1,0:T(8,128)(2,1)} %param.8) | copy-start | bytes 6291460
  11.7 37.7 %all-to-all-start = ((s32[64,1,2]{2,1,0:T(1,128)}), s32[64,1,2]{2,1,0:T(1,128)S(1)}, u32[]{:S(2)}, u32[]{:S(2)}) async-start(s32[64,1,2]{2,1,0:T(1,128)} %bitcast.26), calls=%async_computation.1 | async-start | bytes 65536 | tf_op jit(solution)/shard_map/all_to_all | solution.py:48
  49.4 15.6 %copy-start.2 = (s32[16,2]{0,1:T(2,128)S(1)}, s32[16,2]{0,1:T(2,128)}, u32[]{:S(2)}) copy-start(s32[16,2]{0,1:T(2,128)} %param.7) | copy-start | bytes 388
  49.4 190.0 %all-to-all-start.1 = ((f32[16,64,2,256]{3,2,0,1:T(2,128)}), f32[16,64,2,256]{3,2,0,1:T(2,128)}, u32[]{:S(2)}, u32[]{:S(2)}) async-start(f32[16,64,2,256]{3,2,0,1:T(2,128)} %copy.25), calls=%async_computation.2 | async-start | bytes 4194304 | tf_op jit(solution)/shard_map/all_to_all | solution.py:68
  64.9 3.2 %copy-start.1 = (bf16[16,1024]{1,0:T(8,128)(2,1)S(1)}, bf16[16,1024]{1,0:T(8,128)(2,1)}, u32[]{:S(2)}) copy-start(bf16[16,1024]{1,0:T(8,128)(2,1)} %param.6) | copy-start | bytes 98308
  64.9 38.1 %reduce-scatter.2.cloned.1.call-start = ((), (), s32[]{:S(2)}) async-start(), calls=%async_computation.3 | async-start | bytes 294912 | tf_op jit(solution)/shard_map/reduce_scatter | solution.py:36
  67.5 162.5 %all-gather.2.cloned.1.call-start = ((), (), s32[]{:S(2)}) async-start(), calls=%async_computation.4 | async-start | bytes 2129920 | tf_op jit(solution)/shard_map/all_gather | solution.py:51
Sparse Core Ops, SparseCore 0:
  68.5 34.4 reduce-scatter.1
Sparse Core Ops, SparseCore 1:
  71.3 158.6 all-gather.1
where the time goes:
time: 259 us; the launch traced here: 258 us
  waiting for transfers between devices  147 us (57%)
  local copies, waits for them, and re-layouts  36.1 us (14%)
  starting transfers between devices  34.3 us (13%)
  between operations  15 us (6%)
  blocking collectives  11.8 us (5%)
  matrix products  10 us (4%)
  other arithmetic  3.5 us (1%)
    all_gather x1, waiting for transfers between devices, on_device(): lax.all_gather(sources, 'owner', axis=1, tiled=True)  126 us
    reduce_scatter x1, waiting for transfers between devices, on_device(): lax.psum_scatter(spread.astype(jnp.bfloat16), 'grp', scatter_dimension=1,...  20.5 us
    all_to_all x1, starting transfers between devices, on_device(): lax.all_to_all(wanted.reshape(n_owner, CAP), 'owner', split_axis=0, conca...  18.7 us
    all_to_all x1, starting transfers between devices, on_device(): lax.all_to_all(outgoing.reshape(rhs, n_owner, CAP, P_SIZE), 'owner', spli...  15.5 us
    all_gather x1, blocking collectives, on_device(): lax.all_gather(sources, 'grp', axis=1, tiled=True)  11.8 us
    scatter x1, local copies, waits for them, and re-layouts, on_device(): jnp.zeros((rhs, slot_count, P_SIZE), jnp.float32).at[:, slot]  8.14 us
  transfers between devices with their start and end apart: 4, of which 2 were waited for; matrix products, arithmetic and copies ran while one was open for 13% of the time, Pallas kernels for 0%

commit v1 on v0

v1 whole, which is shorter than its diff:
```python
import jax
import jax.numpy as jnp
from jax import lax
from jax.experimental import pallas as pl
from jax.experimental.pallas import tpu as pltpu
from jax.sharding import Mesh
from jax.sharding import PartitionSpec as P

RHS = 16
PANELS = 256
RANK = 32
CAP = 2
CL = 4
NY = 4
NZH = 8
NZL = 2
NX = 4
NC = 2
GRP = NX * NC
PEERS = NY * NZL
SLOTS = NZH * CAP
NEAR = 16
FAR = 64
BATCH = 8
GROUPS = FAR // BATCH
ROWS = BATCH * RHS
F32 = jnp.float32
BF16 = jnp.bfloat16

VMEM = pl.BlockSpec(memory_space=pltpu.VMEM)
SMEM = pl.BlockSpec(memory_space=pltpu.SMEM)
ANY = pl.BlockSpec(memory_space=pl.ANY)
WHOLE = pl.BlockSpec()


def call(kernel, out_shape, in_specs, out_specs, scratch=(), cost=(0, 0)):
    return pl.pallas_call(
        kernel,
        out_shape=out_shape,
        in_specs=in_specs,
        out_specs=out_specs,
        scratch_shapes=list(scratch),
        compiler_params=pltpu.CompilerParams(vmem_limit_bytes=24 * 1024 * 1024),
        cost_estimate=pl.CostEstimate(flops=cost[0], bytes_accessed=cost[1], transcendentals=0),
    )


def dot_nt(a, b):
    return lax.dot_general(a, b, (((1,), (1,)), ((), ())), preferred_element_type=F32)


def dot_nn(a, b):
    return lax.dot_general(a, b, (((1,), (0,)), ((), ())), preferred_element_type=F32)


def diagonal_mask():
    row = lax.broadcasted_iota(jnp.int32, (ROWS, PANELS), 0) // RHS
    col = lax.broadcasted_iota(jnp.int32, (ROWS, PANELS), 1) // RANK
    return row == col


def spread_kernel(x_ref, out_ref, local_ref):
    for c in range(CL):
        block = x_ref[:, c * PANELS:(c + 1) * PANELS]
        local_ref[c] = block
        for d in range(out_ref.shape[0]):
            out_ref[d, c] = block


def backward_kernel(
    near_ref, far_ref, x_ref, blocks_hbm, left_hbm, right_hbm,
    near_hbm, far_hbm, slot_out,
    count, table, near_sum, blocks_ref, left_ref, right_ref, near_out, far_out, sems,
):
    loads = [
        pltpu.make_async_copy(left_hbm, left_ref, sems.at[0]),
        pltpu.make_async_copy(right_hbm, right_ref, sems.at[1]),
        pltpu.make_async_copy(blocks_hbm, blocks_ref, sems.at[2]),
    ]
    for load in loads:
        load.start()

    def clear(o, _):
        count[o] = 0
        return 0

    lax.fori_loop(0, NY * NZH * NZL, clear, 0)
    table[...] = jnp.zeros(table.shape, F32)
    far_out[...] = jnp.zeros(far_out.shape, BF16)

    def place(n, _):
        source = far_ref[1, n]
        owner = source // (GRP * CL)
        order = count[owner]
        count[owner] = order + 1
        y = owner // (NZH * NZL)
        zh = (owner // NZL) % NZH
        zl = owner % NZL
        peer = y * NZL + zl
        within = zh * CAP + order
        slot_out[n] = peer * (SLOTS + 1) + within
        table[pl.ds(peer * SLOTS + within, 1), :] = jnp.full((1, PANELS), (source % CL).astype(F32))
        return 0

    lax.fori_loop(0, FAR, place, 0)
    for m in range(PEERS):
        far_out[m * (SLOTS + 1) + SLOTS] = table[m * SLOTS:(m + 1) * SLOTS, :].astype(BF16)
    loads[0].wait()
    loads[1].wait()
    mask = diagonal_mask()
    for g in range(GROUPS):
        xt = jnp.concatenate(
            [x_ref[far_ref[0, g * BATCH + i] % CL] for i in range(BATCH)], axis=0
        )
        left = left_ref[g * BATCH:(g + 1) * BATCH].reshape(BATCH * RANK, PANELS)
        right = right_ref[g * BATCH:(g + 1) * BATCH].reshape(BATCH * RANK, PANELS)
        coef = jnp.where(mask, dot_nt(xt, left), 0.0).astype(BF16)
        term = dot_nn(coef, right).astype(BF16)
        for i in range(BATCH):
            far_out[slot_out[g * BATCH + i]] = term[i * RHS:(i + 1) * RHS, :]
    far_store = pltpu.make_async_copy(far_out, far_hbm, sems.at[3])
    far_store.start()
    near_sum[...] = jnp.zeros(near_sum.shape, F32)
    loads[2].wait()
    for n in range(NEAR):
        source = near_ref[1, n] % (GRP * CL)
        near_sum[source] += dot_nn(x_ref[near_ref[0, n] % CL], blocks_ref[n])
    for d in range(GRP):
        near_out[d, 0] = x_ref[...]
        near_out[d, 1] = near_sum[d * CL:(d + 1) * CL].astype(BF16)
    near_store = pltpu.make_async_copy(near_out, near_hbm, sems.at[4])
    near_store.start()
    far_store.wait()
    near_store.wait()


def pick_kernel(x_ref, table_ref, out_ref):
    def peer(m, _):
        table = table_ref[m, SLOTS].astype(F32)
        for s in range(SLOTS):
            want = jnp.broadcast_to(table[s:s + 1, :], (RHS, PANELS))
            block = x_ref[s // CAP, 0].astype(F32)
            for c in range(1, CL):
                block = jnp.where(want == c, x_ref[s // CAP, c].astype(F32), block)
            out_ref[m, s] = block.astype(BF16)
        return 0

    lax.fori_loop(0, PEERS, peer, 0)


def merge_kernel(in_ref, out_ref):
    tables = [in_ref[m, SLOTS].astype(F32) for m in range(PEERS)]
    for zh in range(NZH):
        sums = [jnp.zeros((RHS, PANELS), F32) for _ in range(CL)]
        for m in range(PEERS):
            for s in range(zh * CAP, (zh + 1) * CAP):
                block = in_ref[m, s].astype(F32)
                want = jnp.broadcast_to(tables[m][s:s + 1, :], (RHS, PANELS))
                for c in range(CL):
                    sums[c] = sums[c] + jnp.where(want == c, block, 0.0)
        for c in range(CL):
            out_ref[zh, c] = sums[c].astype(BF16)


def near_kernel(near_ref, got_ref, blocks_ref, out_ref):
    for c in range(CL):
        total = got_ref[0, 1, c].astype(F32)
        for d in range(1, GRP):
            total = total + got_ref[d, 1, c].astype(F32)
        out_ref[c] = total
    for n in range(NEAR):
        source = near_ref[1, n] % (GRP * CL)
        block = got_ref[source // CL, 0, source % CL]
        out_ref[near_ref[0, n] % CL] += dot_nt(block, blocks_ref[n])


def far_kernel(far_ref, slot_ref, x_ref, left_ref, right_ref, out_ref, spread):
    mask = diagonal_mask()
    total = jnp.zeros((CL * RHS, PANELS), F32)
    spread[...] = jnp.zeros(spread.shape, F32)
    for g in range(GROUPS):
        slots = [slot_ref[g * BATCH + i] for i in range(BATCH)]
        xs = jnp.concatenate([x_ref[s - s // (SLOTS + 1)] for s in slots], axis=0)
        left = left_ref[g * BATCH:(g + 1) * BATCH].reshape(BATCH * RANK, PANELS)
        right = right_ref[g * BATCH:(g + 1) * BATCH].reshape(BATCH * RANK, PANELS)
        coef = jnp.where(mask, dot_nt(xs, right), 0.0)
        for i in range(BATCH):
            target = far_ref[0, g * BATCH + i] % CL
            spread[g, target] += coef[i * RHS:(i + 1) * RHS, :]
        total = total + dot_nn(spread[g].reshape(CL * RHS, PANELS).astype(BF16), left)
    out_ref[...] = total.reshape(CL, RHS, PANELS)


def final_kernel(near_ref, far_ref, far_in, out_ref):
    for c in range(CL):
        total = near_ref[c] + far_ref[c]
        for z in range(NZH):
            total = total + far_in[z, c].astype(F32)
        out_ref[:, c * PANELS:(c + 1) * PANELS] = total.astype(BF16)


def shape(dims, dtype=BF16):
    return jax.ShapeDtypeStruct(dims, dtype)


def on_device(sources, near_pairs, near_blocks, far_pairs, far_left, far_right):
    near_table = near_pairs.T
    far_table = far_pairs.T
    spread, local = call(
        spread_kernel,
        (shape((NZH, CL, RHS, PANELS)), shape((CL, RHS, PANELS))),
        [VMEM],
        (WHOLE, VMEM),
        cost=(0, 300000),
    )(sources)
    along_z = lax.all_to_all(spread, "zh", 0, 0, tiled=True)
    near_send, far_send, slots = call(
        backward_kernel,
        (
            shape((GRP, 2, CL, RHS, PANELS)),
            shape((PEERS * (SLOTS + 1), RHS, PANELS)),
            shape((FAR,), jnp.int32),
        ),
        [SMEM, SMEM, VMEM, ANY, ANY, ANY],
        (ANY, ANY, SMEM),
        [
            pltpu.SMEM((NY * NZH * NZL,), jnp.int32),
            pltpu.VMEM((PEERS * SLOTS, PANELS), F32),
            pltpu.VMEM((GRP * CL, RHS, PANELS), F32),
            pltpu.VMEM(near_blocks.shape, BF16),
            pltpu.VMEM(far_left.shape, BF16),
            pltpu.VMEM(far_right.shape, BF16),
            pltpu.VMEM((GRP, 2, CL, RHS, PANELS), BF16),
            pltpu.VMEM((PEERS * (SLOTS + 1), RHS, PANELS), BF16),
            pltpu.SemaphoreType.DMA((5,)),
        ],
        cost=(2000000000, 6000000),
    )(near_table, far_table, local, near_blocks, far_left, far_right)
    region = lax.all_to_all(near_send, ("x", "c"), 0, 0, tiled=True)
    far_got = lax.all_to_all(
        far_send.reshape(PEERS, SLOTS + 1, RHS, PANELS), ("y", "zl"), 0, 0, tiled=True
    )
    picked = call(
        pick_kernel,
        shape((PEERS, SLOTS, RHS, PANELS)),
        [VMEM, VMEM],
        WHOLE,
        cost=(0, 2000000),
    )(along_z, far_got)
    far_sources = lax.all_to_all(picked, ("y", "zl"), 0, 0, tiled=True)
    merged = call(
        merge_kernel, shape((NZH, CL, RHS, PANELS)), [VMEM], WHOLE, cost=(0, 2000000)
    )(far_got)
    far_back = lax.all_to_all(merged, "zh", 0, 0, tiled=True)
    near_total = call(
        near_kernel,
        shape((CL, RHS, PANELS), F32),
        [SMEM, VMEM, VMEM],
        VMEM,
        cost=(500000000, 2500000),
    )(near_table, region, near_blocks)
    far_total = call(
        far_kernel,
        shape((CL, RHS, PANELS), F32),
        [SMEM, SMEM, VMEM, VMEM, VMEM],
        VMEM,
        [pltpu.VMEM((GROUPS, CL, RHS, PANELS), F32)],
        cost=(1000000000, 3500000),
    )(far_table, slots, far_sources.reshape(PEERS * SLOTS, RHS, PANELS), far_left, far_right)
    return call(
        final_kernel, shape(sources.shape), [VMEM] * 3, VMEM, cost=(0, 1000000)
    )(near_total, far_total, far_back)


def solution(mesh):
    axes = ("y", "zh", "zl", "x", "c")
    fine = Mesh(mesh.devices.reshape(NY, NZH, NZL, NX, NC), axes)
    placed = (
        P(None, axes),
        P(axes, None),
        P(axes, None, None),
        P(axes, None),
        P(axes, None, None),
        P(axes, None, None),
    )
    return jax.shard_map(
        on_device, mesh=fine, in_specs=placed, out_specs=P(None, axes), check_vma=False
    )
```

time: 259 us -> 117 us (0.45)
  the two profiles are of different devices: /device:TPU:4 before, /device:TPU:2 now
where the time goes in v1:
time: 117 us; the launch traced here: 116 us
  waiting for transfers between devices  46 us (39%)
  starting transfers between devices  31.4 us (27%)
  blocking collectives  16.4 us (14%)
  Pallas kernels  14.1 us (12%)
  local copies, waits for them, and re-layouts  8.08 us (7%)
    all_to_all x1, blocking collectives, on_device(): lax.all_to_all(far_send.reshape(PEERS, SLOTS + 1, RHS, PANELS), ('y', 'zl...  16.4 us
    all_to_all x1, waiting for transfers between devices, on_device(): far_back = lax.all_to_all(merged, 'zh', 0, 0, tiled=True)  15.4 us
    all_to_all x1, starting transfers between devices, on_device(): along_z = lax.all_to_all(spread, 'zh', 0, 0, tiled=True)  15.1 us
    all_to_all x1, waiting for transfers between devices, on_device(): far_sources = lax.all_to_all(picked, ('y', 'zl'), 0, 0, tiled=True)  14.2 us
    all_to_all x1, waiting for transfers between devices, on_device(): along_z = lax.all_to_all(spread, 'zh', 0, 0, tiled=True)  9.05 us
    unnamed x22, local copies, waits for them, and re-layouts  8.08 us
    all_to_all x1, starting transfers between devices, on_device(): far_back = lax.all_to_all(merged, 'zh', 0, 0, tiled=True)  7.89 us
    all_to_all x1, waiting for transfers between devices, on_device(): region = lax.all_to_all(near_send, ('x', 'c'), 0, 0, tiled=True)  7.37 us
  transfers between devices with their start and end apart: 4, of which 4 were waited for; matrix products, arithmetic and copies ran while one was open for 0% of the time, Pallas kernels for 11%

profile of v1, /device:TPU:2, one launch (start us, length us, event | category | flops | bytes accessed | tf_op | source)
XLA Modules:
  0.0 116.0 jit_solution(12443817284340533291)
XLA Ops:
  0.0 0.0 copy-start.2
  0.0 0.8 copy-done.2
  0.8 0.7 shard_map.64
  1.5 15.1 %all-to-all-start.1 = ((bf16[8,4,16,256]{3,2,1,0:T(8,128)(2,1)}), bf16[8,4,16,256]{3,2,1,0:T(8,128)(2,1)S(1)}, u32[]{:S(2)}, u32[]{:S(2)}) async-start(bf16[8,4,16,256]{3,2,1,0:T(8,128)(2,1)} %get-tuple-element.13), calls=%async_computation.1 | async-start | bytes 524288 | tf_op jit(solution)/shard_map/all_to_all | solution.py:216
  16.6 0.0 copy-start
  16.6 1.6 %copy-done = bf16[16,256,256]{2,1,0:T(8,128)(2,1)S(1)} copy-done((bf16[16,256,256]{2,1,0:T(8,128)(2,1)S(1)}, bf16[16,256,256]{2,1,0:T(8,128)(2,1)}, u32[]{:S(2)}) %copy-start) | copy-done | bytes 2097176
  18.2 0.0 copy-start.3
  18.2 0.7 copy-done.3
  18.8 0.0 copy-start.5
  18.8 1.2 %copy-done.5 = bf16[64,32,256]{2,1,0:T(8,128)(2,1)S(1)} copy-done((bf16[64,32,256]{2,1,0:T(8,128)(2,1)S(1)}, bf16[64,32,256]{2,1,0:T(8,128)(2,1)}, u32[]{:S(2)}) %copy-start.5) | copy-done | bytes 1048600
  20.1 0.0 copy-start.7
  20.1 1.2 %copy-done.7 = bf16[64,32,256]{2,1,0:T(8,128)(2,1)S(1)} copy-done((bf16[64,32,256]{2,1,0:T(8,128)(2,1)S(1)}, bf16[64,32,256]{2,1,0:T(8,128)(2,1)}, u32[]{:S(2)}) %copy-start.7) | copy-done | bytes 1048600
  21.3 0.0 copy-start.9
  21.3 0.7 copy-done.9
  22.0 6.9 %shard_map.65 = (bf16[8,2,4,16,256]{4,3,2,1,0:T(8,128)(2,1)}, bf16[136,16,256]{2,1,0:T(8,128)(2,1)S(1)}, s32[64]{0:T(128)S(1)}) custom-call(s32[2,16]{1,0:T(2,128)S(1)} %bitcast.6, s32[2,64]{1,0:T(2,128)S(1)} %bitcast.8, bf16[4,16,256]{2,1,0:T(8,128)(2,1)S(1)} %get-tuple-element.10.x_ref, bf16[16,256,256]{2,1,0:T(8,128)(2,1)S(1)} %copy-done, ...), custom_call_target="tpu_custom_call" | custom-call | flops 2000000000 | bytes 6000000 | tf_op jit(solution)/shard_map/pallas_call | solution.py:217
  28.9 9.1 %all-to-all-done.1.x_ref = bf16[8,4,16,256]{3,2,1,0:T(8,128)(2,1)S(1)} async-done(((bf16[8,4,16,256]{3,2,1,0:T(8,128)(2,1)}), bf16[8,4,16,256]{3,2,1,0:T(8,128)(2,1)S(1)}, u32[]{:S(2)}, u32[]{:S(2)}) %all-to-all-start.1) | async-done | bytes 262176 | tf_op jit(solution)/shard_map/all_to_all | solution.py:216
  37.9 16.4 %all_to_all.25.table_ref.in_ref = bf16[8,17,16,256]{3,2,1,0:T(8,128)(2,1)S(1)} all-to-all(bf16[8,17,16,256]{3,2,1,0:T(8,128)(2,1)S(1)} %bitcast.4), channel_id=1, replica_groups=mesh['y'=4,'zh'=8,'zl'=2,'x'=4,'c'=2] {'y','zl'}, dimensions={0} | all-to-all | bytes 2228224 | tf_op jit(solution)/shard_map/all_to_all | solution.py:240
  54.3 4.8 %all-to-all-start = ((bf16[8,2,4,16,256]{4,3,2,1,0:T(8,128)(2,1)}), bf16[8,2,4,16,256]{4,3,2,1,0:T(8,128)(2,1)S(1)}, u32[]{:S(2)}, u32[]{:S(2)}) async-start(bf16[8,2,4,16,256]{4,3,2,1,0:T(8,128)(2,1)} %get-tuple-element.11), calls=%async_computation | async-start | bytes 1048576 | tf_op jit(solution)/shard_map/all_to_all | solution.py:239
  59.2 1.5 %shard_map.67 = bf16[8,16,16,256]{3,2,1,0:T(8,128)(2,1)} custom-call(bf16[8,4,16,256]{3,2,1,0:T(8,128)(2,1)S(1)} %all-to-all-done.1.x_ref, bf16[8,17,16,256]{3,2,1,0:T(8,128)(2,1)S(1)} %all_to_all.25.table_ref.in_ref), custom_call_target="tpu_custom_call" | custom-call | bytes 2000000 | tf_op jit(solution)/shard_map/pallas_call | solution.py:243
  60.7 7.4 %all-to-all-done.got_ref = bf16[8,2,4,16,256]{4,3,2,1,0:T(8,128)(2,1)S(1)} async-done(((bf16[8,2,4,16,256]{4,3,2,1,0:T(8,128)(2,1)}), bf16[8,2,4,16,256]{4,3,2,1,0:T(8,128)(2,1)S(1)}, u32[]{:S(2)}, u32[]{:S(2)}) %all-to-all-start) | async-done | bytes 524320 | tf_op jit(solution)/shard_map/all_to_all | solution.py:239
  68.0 3.6 %all-to-all-start.3 = ((bf16[8,16,16,256]{3,2,1,0:T(8,128)(2,1)}), bf16[8,16,16,256]{3,2,1,0:T(8,128)(2,1)S(1)}, u32[]{:S(2)}, u32[]{:S(2)}) async-start(bf16[8,16,16,256]{3,2,1,0:T(8,128)(2,1)} %shard_map.67), calls=%async_computation.3 | async-start | bytes 2097152 | tf_op jit(solution)/shard_map/all_to_all | solution.py:250
  71.6 0.0 copy-start.4
  71.6 1.6 %shard_map.69 = bf16[8,4,16,256]{3,2,1,0:T(8,128)(2,1)} custom-call(bf16[8,17,16,256]{3,2,1,0:T(8,128)(2,1)S(1)} %all_to_all.25.table_ref.in_ref), custom_call_target="tpu_custom_call" | custom-call | bytes 2000000 | tf_op jit(solution)/shard_map/pallas_call | solution.py:251
  73.2 14.2 %all-to-all-done.3 = bf16[8,16,16,256]{3,2,1,0:T(8,128)(2,1)S(1)} async-done(((bf16[8,16,16,256]{3,2,1,0:T(8,128)(2,1)}), bf16[8,16,16,256]{3,2,1,0:T(8,128)(2,1)S(1)}, u32[]{:S(2)}, u32[]{:S(2)}) %all-to-all-start.3) | async-done | bytes 1048608 | tf_op jit(solution)/shard_map/all_to_all | solution.py:250
  87.4 7.9 %all-to-all-start.4 = ((bf16[8,4,16,256]{3,2,1,0:T(8,128)(2,1)}), bf16[8,4,16,256]{3,2,1,0:T(8,128)(2,1)S(1)}, u32[]{:S(2)}, u32[]{:S(2)}) async-start(bf16[8,4,16,256]{3,2,1,0:T(8,128)(2,1)} %shard_map.69), calls=%async_computation.4 | async-start | bytes 524288 | tf_op jit(solution)/shard_map/all_to_all | solution.py:254
  95.3 0.0 copy-done.4
  95.3 0.0 copy-start.1
  95.3 1.6 %copy-done.1 = bf16[16,256,256]{2,1,0:T(8,128)(2,1)S(1)} copy-done((bf16[16,256,256]{2,1,0:T(8,128)(2,1)S(1)}, bf16[16,256,256]{2,1,0:T(8,128)(2,1)}, u32[]{:S(2)}) %copy-start.1) | copy-done | bytes 2097176
  96.9 0.0 copy-start.6
  96.9 0.0 copy-start.8
  96.9 0.0 copy-start.10
  96.9 1.2 %shard_map.66.near_ref = f32[4,16,256]{2,1,0:T(8,128)S(1)} custom-call(s32[2,16]{1,0:T(2,128)S(1)} %bitcast.7, bf16[8,2,4,16,256]{4,3,2,1,0:T(8,128)(2,1)S(1)} %all-to-all-done.got_ref, bf16[16,256,256]{2,1,0:T(8,128)(2,1)S(1)} %copy-done.1), custom_call_target="tpu_custom_call" | custom-call | flops 500000000 | bytes 2500000 | tf_op jit(solution)/shard_map/pallas_call | solution.py:255
  98.1 0.0 copy-done.6
  98.1 0.3 copy-done.8
  98.4 0.0 copy-done.10
  98.4 1.5 %shard_map.68.far_ref = f32[4,16,256]{2,1,0:T(8,128)S(1)} custom-call(s32[2,64]{1,0:T(2,128)S(1)} %bitcast.9, s32[64]{0:T(128)S(1)} %get-tuple-element.12.slot_ref, bf16[128,16,256]{2,1,0:T(8,128)(2,1)S(1)} %bitcast.5, bf16[64,32,256]{2,1,0:T(8,128)(2,1)S(1)} %copy-done.6, bf16[64,32,256]{2,1,0:T(8,128)(2,1)S(1)} %copy-done.8), custom_call_target="tpu_custom_call" | custom-call | flops 1000000000 | bytes 3500000 | tf_op jit(solution)/shard_map/pallas_call | solution.py:262
  99.9 15.4 %all-to-all-done.4.far_in = bf16[8,4,16,256]{3,2,1,0:T(8,128)(2,1)S(1)} async-done(((bf16[8,4,16,256]{3,2,1,0:T(8,128)(2,1)}), bf16[8,4,16,256]{3,2,1,0:T(8,128)(2,1)S(1)}, u32[]{:S(2)}, u32[]{:S(2)}) %all-to-all-start.4) | async-done | bytes 262176 | tf_op jit(solution)/shard_map/all_to_all | solution.py:254
  115.3 0.7 shard_map.70
Async XLA Ops:
  0.0 0.8 copy-start.2
  1.5 36.5 %all-to-all-start.1 = ((bf16[8,4,16,256]{3,2,1,0:T(8,128)(2,1)}), bf16[8,4,16,256]{3,2,1,0:T(8,128)(2,1)S(1)}, u32[]{:S(2)}, u32[]{:S(2)}) async-start(bf16[8,4,16,256]{3,2,1,0:T(8,128)(2,1)} %get-tuple-element.13), calls=%async_computation.1 | async-start | bytes 524288 | tf_op jit(solution)/shard_map/all_to_all | solution.py:216
  16.6 1.6 %copy-start = (bf16[16,256,256]{2,1,0:T(8,128)(2,1)S(1)}, bf16[16,256,256]{2,1,0:T(8,128)(2,1)}, u32[]{:S(2)}) copy-start(bf16[16,256,256]{2,1,0:T(8,128)(2,1)} %blocks_ref.1) | copy-start | bytes 6291460
  18.2 0.7 copy-start.3
  18.8 1.2 %copy-start.5 = (bf16[64,32,256]{2,1,0:T(8,128)(2,1)S(1)}, bf16[64,32,256]{2,1,0:T(8,128)(2,1)}, u32[]{:S(2)}) copy-start(bf16[64,32,256]{2,1,0:T(8,128)(2,1)} %left_ref.1) | copy-start | bytes 3145732
  20.1 1.2 %copy-start.7 = (bf16[64,32,256]{2,1,0:T(8,128)(2,1)S(1)}, bf16[64,32,256]{2,1,0:T(8,128)(2,1)}, u32[]{:S(2)}) copy-start(bf16[64,32,256]{2,1,0:T(8,128)(2,1)} %right_ref.1) | copy-start | bytes 3145732
  21.3 0.7 copy-start.9
  54.3 13.7 %all-to-all-start = ((bf16[8,2,4,16,256]{4,3,2,1,0:T(8,128)(2,1)}), bf16[8,2,4,16,256]{4,3,2,1,0:T(8,128)(2,1)S(1)}, u32[]{:S(2)}, u32[]{:S(2)}) async-start(bf16[8,2,4,16,256]{4,3,2,1,0:T(8,128)(2,1)} %get-tuple-element.11), calls=%async_computation | async-start | bytes 1048576 | tf_op jit(solution)/shard_map/all_to_all | solution.py:239
  68.0 19.3 %all-to-all-start.3 = ((bf16[8,16,16,256]{3,2,1,0:T(8,128)(2,1)}), bf16[8,16,16,256]{3,2,1,0:T(8,128)(2,1)S(1)}, u32[]{:S(2)}, u32[]{:S(2)}) async-start(bf16[8,16,16,256]{3,2,1,0:T(8,128)(2,1)} %shard_map.67), calls=%async_computation.3 | async-start | bytes 2097152 | tf_op jit(solution)/shard_map/all_to_all | solution.py:250
  71.6 23.7 %copy-start.4 = (s32[16,2]{0,1:T(2,128)S(1)}, s32[16,2]{0,1:T(2,128)}, u32[]{:S(2)}) copy-start(s32[16,2]{0,1:T(2,128)} %param.7) | copy-start | bytes 388
  87.4 28.0 %all-to-all-start.4 = ((bf16[8,4,16,256]{3,2,1,0:T(8,128)(2,1)}), bf16[8,4,16,256]{3,2,1,0:T(8,128)(2,1)S(1)}, u32[]{:S(2)}, u32[]{:S(2)}) async-start(bf16[8,4,16,256]{3,2,1,0:T(8,128)(2,1)} %shard_map.69), calls=%async_computation.4 | async-start | bytes 524288 | tf_op jit(solution)/shard_map/all_to_all | solution.py:254
  95.3 1.6 %copy-start.1 = (bf16[16,256,256]{2,1,0:T(8,128)(2,1)S(1)}, bf16[16,256,256]{2,1,0:T(8,128)(2,1)}, u32[]{:S(2)}) copy-start(bf16[16,256,256]{2,1,0:T(8,128)(2,1)} %blocks_ref.1) | copy-start | bytes 6291460
  96.9 1.2 %copy-start.6 = (bf16[64,32,256]{2,1,0:T(8,128)(2,1)S(1)}, bf16[64,32,256]{2,1,0:T(8,128)(2,1)}, u32[]{:S(2)}) copy-start(bf16[64,32,256]{2,1,0:T(8,128)(2,1)} %left_ref.1) | copy-start | bytes 3145732
  96.9 1.5 %copy-start.8 = (bf16[64,32,256]{2,1,0:T(8,128)(2,1)S(1)}, bf16[64,32,256]{2,1,0:T(8,128)(2,1)}, u32[]{:S(2)}) copy-start(bf16[64,32,256]{2,1,0:T(8,128)(2,1)} %right_ref.1) | copy-start | bytes 3145732
  96.9 1.5 %copy-start.10 = (s32[64,2]{0,1:T(2,128)S(1)}, s32[64,2]{0,1:T(2,128)}, u32[]{:S(2)}) copy-start(s32[64,2]{0,1:T(2,128)} %param.9) | copy-start | bytes 1540

commit v2 on v1

v2 whole, which is shorter than its diff:
```python
import jax
import jax.numpy as jnp
from jax import lax
from jax.experimental import pallas as pl
from jax.experimental.pallas import tpu as pltpu
from jax.sharding import Mesh
from jax.sharding import PartitionSpec as P

RHS = 16
PANELS = 256
RANK = 32
CAP = 2
CL = 4
NY = 4
NZH = 8
NZL = 2
NX = 4
NC = 2
GRP = NX * NC
PEERS = NY * NZL
SLOTS = NZH * CAP
NEAR = 16
FAR = 64
BATCH = 8
GROUPS = FAR // BATCH
ROWS = BATCH * RHS
F32 = jnp.float32
BF16 = jnp.bfloat16

VMEM = pl.BlockSpec(memory_space=pltpu.VMEM)
SMEM = pl.BlockSpec(memory_space=pltpu.SMEM)
ANY = pl.BlockSpec(memory_space=pl.ANY)
WHOLE = pl.BlockSpec()


def call(kernel, out_shape, in_specs, out_specs, scratch=(), cost=(0, 0), vmem=24):
    return pl.pallas_call(
        kernel,
        out_shape=out_shape,
        in_specs=in_specs,
        out_specs=out_specs,
        scratch_shapes=list(scratch),
        compiler_params=pltpu.CompilerParams(vmem_limit_bytes=vmem * 1024 * 1024),
        cost_estimate=pl.CostEstimate(flops=cost[0], bytes_accessed=cost[1], transcendentals=0),
    )


def dot_nt(a, b):
    return lax.dot_general(a, b, (((1,), (1,)), ((), ())), preferred_element_type=F32)


def dot_nn(a, b):
    return lax.dot_general(a, b, (((1,), (0,)), ((), ())), preferred_element_type=F32)


def diagonal_mask():
    row = lax.broadcasted_iota(jnp.int32, (ROWS, PANELS), 0) // RHS
    col = lax.broadcasted_iota(jnp.int32, (ROWS, PANELS), 1) // RANK
    return row == col


def far_send_kernel(
    far_ref, x_hbm, left_hbm, right_hbm, out_hbm, slot_out,
    count, table, x_ref, left_ref, right_ref, out_ref, sems,
):
    loads = [
        pltpu.make_async_copy(x_hbm, x_ref, sems.at[0]),
        pltpu.make_async_copy(left_hbm, left_ref, sems.at[1]),
        pltpu.make_async_copy(right_hbm, right_ref, sems.at[2]),
    ]
    for load in loads:
        load.start()

    def clear(o, _):
        count[o] = 0
        return 0

    lax.fori_loop(0, NY * NZH * NZL, clear, 0)
    table[...] = jnp.zeros(table.shape, F32)
    out_ref[...] = jnp.zeros(out_ref.shape, BF16)

    def place(n, _):
        source = far_ref[1, n]
        owner = source // (GRP * CL)
        order = count[owner]
        count[owner] = order + 1
        y = owner // (NZH * NZL)
        zh = (owner // NZL) % NZH
        zl = owner % NZL
        peer = y * NZL + zl
        within = zh * CAP + order
        slot_out[n] = peer * (SLOTS + 1) + within
        table[pl.ds(peer * SLOTS + within, 1), :] = jnp.full((1, PANELS), (source % CL).astype(F32))
        return 0

    lax.fori_loop(0, FAR, place, 0)
    for m in range(PEERS):
        out_ref[m * (SLOTS + 1) + SLOTS] = table[m * SLOTS:(m + 1) * SLOTS, :].astype(BF16)
    for load in loads:
        load.wait()
    mask = diagonal_mask()
    for g in range(GROUPS):
        targets = [far_ref[0, g * BATCH + i] % CL for i in range(BATCH)]
        xt = jnp.concatenate(
            [x_ref[:, pl.ds(pl.multiple_of(t * PANELS, PANELS), PANELS)] for t in targets], axis=0
        )
        left = left_ref[g * BATCH:(g + 1) * BATCH].reshape(BATCH * RANK, PANELS)
        right = right_ref[g * BATCH:(g + 1) * BATCH].reshape(BATCH * RANK, PANELS)
        coef = jnp.where(mask, dot_nt(xt, left), 0.0).astype(BF16)
        term = dot_nn(coef, right).astype(BF16)
        for i in range(BATCH):
            out_ref[slot_out[g * BATCH + i]] = term[i * RHS:(i + 1) * RHS, :]
    store = pltpu.make_async_copy(out_ref, out_hbm, sems.at[3])
    store.start()
    store.wait()


def near_send_kernel(near_ref, x_ref, blocks_ref, swap_out, own_out, near_sum):
    x = lax.axis_index("x")
    c = lax.axis_index("c")
    for w in range(CL):
        swap_out[0, w] = x_ref[:, w * PANELS:(w + 1) * PANELS]
    near_sum[...] = jnp.zeros(near_sum.shape, F32)
    for n in range(NEAR):
        source = near_ref[1, n] % (GRP * CL)
        start = pl.multiple_of((near_ref[0, n] % CL) * PANELS, PANELS)
        near_sum[source] += dot_nn(x_ref[:, pl.ds(start, PANELS)], blocks_ref[n])
    for k in range(NX):
        at = ((x + k) % NX) * (NC * CL)
        own_out[k] = near_sum[pl.ds(at + c * CL, CL)]
        swap_out[1 + k] = near_sum[pl.ds(at + (1 - c) * CL, CL)].astype(BF16)


def near_pack_kernel(x_ref, own_ref, got_ref, home_ref, *out_refs):
    home_ref[...] = own_ref[0] + got_ref[1].astype(F32)
    for k in range(1, NX):
        out = out_refs[k - 1]
        for w in range(CL):
            out[0, w] = x_ref[:, w * PANELS:(w + 1) * PANELS]
        out[1] = got_ref[0]
        out[2] = (own_ref[k] + got_ref[1 + k].astype(F32)).astype(BF16)


def pick_kernel(x_ref, table_ref, after_ref, out_ref):
    def peer(m, _):
        table = table_ref[m, SLOTS].astype(F32)
        for s in range(SLOTS):
            want = jnp.broadcast_to(table[s:s + 1, :], (RHS, PANELS))
            block = x_ref[s // CAP, 0, 0].astype(F32)
            for w in range(1, CL):
                block = jnp.where(want == w, x_ref[s // CAP, 0, w].astype(F32), block)
            out_ref[m, s] = block.astype(BF16)
        return 0

    lax.fori_loop(0, PEERS, peer, 0)


def merge_kernel(x_ref, in_ref, out_ref):
    for w in range(CL):
        block = x_ref[:, w * PANELS:(w + 1) * PANELS]
        for zh in range(NZH):
            out_ref[zh, 0, w] = block
    tables = [in_ref[m, SLOTS].astype(F32) for m in range(PEERS)]
    for zh in range(NZH):
        sums = [jnp.zeros((RHS, PANELS), F32) for _ in range(CL)]
        for m in range(PEERS):
            for s in range(zh * CAP, (zh + 1) * CAP):
                block = in_ref[m, s].astype(F32)
                want = jnp.broadcast_to(tables[m][s:s + 1, :], (RHS, PANELS))
                for w in range(CL):
                    sums[w] = sums[w] + jnp.where(want == w, block, 0.0)
        for w in range(CL):
            out_ref[zh, 1, w] = sums[w].astype(BF16)


def near_kernel(near_ref, x_ref, mate_ref, home_ref, *rest):
    got_refs, (blocks_ref, out_ref, region) = rest[:NX - 1], rest[NX - 1:]
    x = lax.axis_index("x")
    c = lax.axis_index("c")
    for w in range(CL):
        region[0, w] = x_ref[:, w * PANELS:(w + 1) * PANELS]
        region[1, w] = mate_ref[0, w]
        total = home_ref[w]
        for k in range(1, NX):
            region[2 * k, w] = got_refs[k - 1][0, w]
            region[2 * k + 1, w] = got_refs[k - 1][1, w]
            total = total + got_refs[k - 1][2, w].astype(F32)
        out_ref[w] = total
    for n in range(NEAR):
        source = near_ref[1, n] % (GRP * CL)
        x_at = source // (NC * CL)
        c_at = (source // CL) % NC
        holder = ((x - x_at + NX) % NX) * NC + (c_at + c) % NC
        out_ref[near_ref[0, n] % CL] += dot_nt(region[holder, source % CL], blocks_ref[n])


def far_kernel(
    far_ref, slot_ref, x_ref, left_ref, right_ref, near_ref, back_ref, out_ref, spread
):
    mask = diagonal_mask()
    total = near_ref[...]
    for z in range(NZH):
        total = total + back_ref[z, 1].astype(F32)
    total = total.reshape(CL * RHS, PANELS)
    spread[...] = jnp.zeros(spread.shape, F32)
    for g in range(GROUPS):
        slots = [slot_ref[g * BATCH + i] for i in range(BATCH)]
        xs = jnp.concatenate([x_ref[s - s // (SLOTS + 1)] for s in slots], axis=0)
        left = left_ref[g * BATCH:(g + 1) * BATCH].reshape(BATCH * RANK, PANELS)
        right = right_ref[g * BATCH:(g + 1) * BATCH].reshape(BATCH * RANK, PANELS)
        coef = jnp.where(mask, dot_nt(xs, right), 0.0)
        for i in range(BATCH):
            target = far_ref[0, g * BATCH + i] % CL
            spread[g, target] += coef[i * RHS:(i + 1) * RHS, :]
        total = total + dot_nn(spread[g].reshape(CL * RHS, PANELS).astype(BF16), left)
    for w in range(CL):
        out_ref[:, w * PANELS:(w + 1) * PANELS] = total[w * RHS:(w + 1) * RHS].astype(BF16)


def shape(dims, dtype=BF16):
    return jax.ShapeDtypeStruct(dims, dtype)


def shift(array, axis, size, by):
    return lax.ppermute(array, axis, [(i, (i + by) % size) for i in range(size)])


def on_device(sources, near_pairs, near_blocks, far_pairs, far_left, far_right):
    near_table = near_pairs.T
    far_table = far_pairs.T
    block = (CL, RHS, PANELS)
    far_send, slots = call(
        far_send_kernel,
        (shape((PEERS * (SLOTS + 1), RHS, PANELS)), shape((FAR,), jnp.int32)),
        [SMEM, ANY, ANY, ANY],
        (ANY, SMEM),
        [
            pltpu.SMEM((NY * NZH * NZL,), jnp.int32),
            pltpu.VMEM((PEERS * SLOTS, PANELS), F32),
            pltpu.VMEM(sources.shape, BF16),
            pltpu.VMEM(far_left.shape, BF16),
            pltpu.VMEM(far_right.shape, BF16),
            pltpu.VMEM((PEERS * (SLOTS + 1), RHS, PANELS), BF16),
            pltpu.SemaphoreType.DMA((4,)),
        ],
        cost=(1000000000, 3500000),
        vmem=60,
    )(far_table, sources, far_left, far_right)
    far_got = lax.all_to_all(
        far_send.reshape(PEERS, SLOTS + 1, RHS, PANELS), ("y", "zl"), 0, 0, tiled=True
    )
    swap, own = call(
        near_send_kernel,
        (shape((1 + NX, *block)), shape((NX, *block), F32)),
        [SMEM, VMEM, VMEM],
        (VMEM, VMEM),
        [pltpu.VMEM((GRP * CL, RHS, PANELS), F32)],
        cost=(1000000000, 3500000),
    )(near_table, sources, near_blocks)
    mate = shift(swap, "c", NC, 1)
    home, *packs = call(
        near_pack_kernel,
        (shape(block, F32),) + (shape((3, *block)),) * (NX - 1),
        [VMEM] * 3,
        (VMEM,) * NX,
        cost=(0, 1000000),
    )(sources, own, mate)
    got = [shift(pack, "x", NX, k + 1) for k, pack in enumerate(packs)]
    near_total = call(
        near_kernel,
        shape(block, F32),
        [SMEM] + [VMEM] * (NX + 3),
        VMEM,
        [pltpu.VMEM((GRP, *block), BF16)],
        cost=(500000000, 2500000),
    )(near_table, sources, mate, home, *got, near_blocks)
    merged = call(
        merge_kernel, shape((NZH, 2, *block)), [VMEM, VMEM], WHOLE, cost=(0, 2000000)
    )(sources, far_got)
    along_z = lax.all_to_all(merged, "zh", 0, 0, tiled=True)
    picked = call(
        pick_kernel,
        shape((PEERS, SLOTS, RHS, PANELS)),
        [VMEM, VMEM, ANY],
        WHOLE,
        cost=(0, 2000000),
    )(along_z, far_got, near_total)
    far_sources = lax.all_to_all(picked, ("y", "zl"), 0, 0, tiled=True)
    return call(
        far_kernel,
        shape(sources.shape),
        [SMEM, SMEM] + [VMEM] * 5,
        VMEM,
        [pltpu.VMEM((GROUPS, *block), F32)],
        cost=(1000000000, 3500000),
    )(
        far_table, slots, far_sources.reshape(PEERS * SLOTS, RHS, PANELS),
        far_left, far_right, near_total, along_z,
    )


def solution(mesh):
    axes = ("y", "zh", "zl", "x", "c")
    fine = Mesh(mesh.devices.reshape(NY, NZH, NZL, NX, NC), axes)
    placed = (
        P(None, axes),
        P(axes, None),
        P(axes, None, None),
        P(axes, None),
        P(axes, None, None),
        P(axes, None, None),
    )
    return jax.shard_map(
        on_device, mesh=fine, in_specs=placed, out_specs=P(None, axes), check_vma=False
    )
```

time: 117 us -> 95.6 us (0.82)
  the two profiles are of different devices: /device:TPU:2 before, /device:TPU:64 now
where the time goes in v2:
time: 95.6 us; the launch traced here: 95.1 us
  blocking collectives  40.9 us (43%)
  starting transfers between devices  27.1 us (28%)
  Pallas kernels  12.9 us (13%)
  waiting for transfers between devices  12.5 us (13%)
  local copies, waits for them, and re-layouts  1.63 us (2%)
    all_to_all x1, blocking collectives, on_device(): lax.all_to_all(far_send.reshape(PEERS, SLOTS + 1, RHS, PANELS), ('y', 'zl...  22.4 us
    all_to_all x1, blocking collectives, on_device(): far_sources = lax.all_to_all(picked, ('y', 'zl'), 0, 0, tiled=True)  18.4 us
    all_to_all x1, starting transfers between devices, on_device(): along_z = lax.all_to_all(merged, 'zh', 0, 0, tiled=True)  13.8 us
    ppermute x4, starting transfers between devices, shift(): lax.ppermute(array, axis, [(i, (i + by) % size) for i in range(size)])  13.3 us
    all_to_all x1, waiting for transfers between devices, on_device(): along_z = lax.all_to_all(merged, 'zh', 0, 0, tiled=True)  7.97 us
    pallas_call x1, Pallas kernels, on_device(): call(far_send_kernel, (shape((PEERS * (SLOTS + 1), RHS, PANELS)), shape((...  6.25 us
    ppermute x4, waiting for transfers between devices, shift(): lax.ppermute(array, axis, [(i, (i + by) % size) for i in range(size)])  4.51 us
    pallas_call x1, Pallas kernels, on_device(): call(far_kernel, shape(sources.shape), [SMEM, SMEM] + [VMEM] * 5, VMEM, [...  2.27 us
  transfers between devices with their start and end apart: 5, of which 3 were waited for; matrix products, arithmetic and copies ran while one was open for 0% of the time, Pallas kernels for 2%

profile of v2, /device:TPU:64, one launch (start us, length us, event | category | flops | bytes accessed | tf_op | source)
XLA Modules:
  0.0 95.1 jit_solution(18262150356993957613)
XLA Ops:
  0.0 6.3 %shard_map.64 = (bf16[136,16,256]{2,1,0:T(8,128)(2,1)}, s32[64]{0:T(128)}) custom-call(s32[2,64]{1,0:T(2,128)} %bitcast.7, bf16[16,1024]{1,0:T(8,128)(2,1)} %x_ref.7, bf16[64,32,256]{2,1,0:T(8,128)(2,1)} %left_ref.1, bf16[64,32,256]{2,1,0:T(8,128)(2,1)} %right_ref.1), custom_call_target="tpu_custom_call" | custom-call | flops 1000000000 | bytes 3500000 | tf_op jit(solution)/shard_map/pallas_call | solution.py:232
  6.3 0.0 copy-start.4
  6.3 22.4 %all_to_all.15.in_ref.table_ref = bf16[8,17,16,256]{3,2,1,0:T(8,128)(2,1)S(1)} all-to-all(bf16[8,17,16,256]{3,2,1,0:T(8,128)(2,1)} %bitcast.9), channel_id=1, replica_groups=mesh['y'=4,'zh'=8,'zl'=2,'x'=4,'c'=2] {'y','zl'}, dimensions={0} | all-to-all | bytes 2228224 | tf_op jit(solution)/shard_map/all_to_all | solution.py:249
  28.7 0.0 copy-done.4
  28.7 0.0 copy-start.5
  28.7 1.7 %shard_map.65 = bf16[8,2,4,16,256]{4,3,2,1,0:T(8,128)(2,1)} custom-call(bf16[16,1024]{1,0:T(8,128)(2,1)S(1)} %copy-done.4, bf16[8,17,16,256]{3,2,1,0:T(8,128)(2,1)S(1)} %all_to_all.15.in_ref.table_ref), custom_call_target="tpu_custom_call" | custom-call | bytes 2000000 | tf_op jit(solution)/shard_map/pallas_call | solution.py:277
  30.4 13.8 %all-to-all-start.1 = ((bf16[8,2,4,16,256]{4,3,2,1,0:T(8,128)(2,1)}), bf16[8,2,4,16,256]{4,3,2,1,0:T(8,128)(2,1)S(1)}, u32[]{:S(2)}, u32[]{:S(2)}) async-start(bf16[8,2,4,16,256]{4,3,2,1,0:T(8,128)(2,1)} %shard_map.65), calls=%async_computation.1 | async-start | bytes 1048576 | tf_op jit(solution)/shard_map/all_to_all | solution.py:280
  44.2 0.0 copy-done.5
  44.2 0.0 copy-start
  44.2 1.6 %copy-done = bf16[16,256,256]{2,1,0:T(8,128)(2,1)S(1)} copy-done((bf16[16,256,256]{2,1,0:T(8,128)(2,1)S(1)}, bf16[16,256,256]{2,1,0:T(8,128)(2,1)}, u32[]{:S(2)}) %copy-start) | copy-done | bytes 2097176
  45.8 0.0 copy-start.1
  45.8 1.0 %shard_map.66 = (bf16[5,4,16,256]{3,2,1,0:T(8,128)(2,1)S(1)}, f32[4,4,16,256]{3,2,1,0:T(8,128)S(1)}) custom-call(s32[2,16]{1,0:T(2,128)S(1)} %bitcast.5, bf16[16,1024]{1,0:T(8,128)(2,1)S(1)} %copy-done.4, bf16[16,256,256]{2,1,0:T(8,128)(2,1)S(1)} %copy-done), custom_call_target="tpu_custom_call" | custom-call | flops 1000000000 | bytes 3500000 | tf_op jit(solution)/shard_map/pallas_call | solution.py:252
  46.8 1.9 %collective-permute-start = (bf16[5,4,16,256]{3,2,1,0:T(8,128)(2,1)S(1)}, bf16[5,4,16,256]{3,2,1,0:T(8,128)(2,1)S(1)}, u32[]{:S(2)}, u32[]{:S(2)}) collective-permute-start(bf16[5,4,16,256]{3,2,1,0:T(8,128)(2,1)S(1)} %get-tuple-element.15), channel_id=1, source_target_pairs={{0,1},{1,0},{2,3},{3,2},{4,5},{5,4},{6,7},{7,6},{8,9},{9,8},{10,11... | collective-permute-start | bytes 491528 | tf_op jit(solution)/shard_map/ppermute | solution.py:225
  48.7 1.4 %collective-permute-done.got_ref.mate_ref = bf16[5,4,16,256]{3,2,1,0:T(8,128)(2,1)S(1)} collective-permute-done((bf16[5,4,16,256]{3,2,1,0:T(8,128)(2,1)S(1)}, bf16[5,4,16,256]{3,2,1,0:T(8,128)(2,1)S(1)}, u32[]{:S(2)}, u32[]{:S(2)}) %collective-permute-start) | collective-permute-done | bytes 163872 | tf_op jit(solution)/shard_map/ppermute | solution.py:225
  50.1 3.4 %collective-permute-start.1 = (bf16[3,4,16,256]{3,2,1,0:T(8,128)(2,1)S(1)}, bf16[3,4,16,256]{3,2,1,0:T(8,128)(2,1)S(1)}, u32[]{:S(2)}, u32[]{:S(2)}) collective-permute-start(bf16[3,4,16,256]{3,2,1,0:T(8,128)(2,1)S(1)} %get-tuple-element.18), channel_id=1, source_target_pairs={{0,2},{2,4},{4,6},{6,0},{1,3},{3,5},{5,7},{7,1},{8,10},{10,12},{12... | collective-permute-start | bytes 294920 | tf_op jit(solution)/shard_map/ppermute | solution.py:225
  53.5 4.6 %collective-permute-start.2 = (bf16[3,4,16,256]{3,2,1,0:T(8,128)(2,1)S(1)}, bf16[3,4,16,256]{3,2,1,0:T(8,128)(2,1)S(1)}, u32[]{:S(2)}, u32[]{:S(2)}) collective-permute-start(bf16[3,4,16,256]{3,2,1,0:T(8,128)(2,1)S(1)} %get-tuple-element.19), channel_id=1, source_target_pairs={{0,4},{2,6},{4,0},{6,2},{1,5},{3,7},{5,1},{7,3},{8,12},{10,14},{12... | collective-permute-start | bytes 294920 | tf_op jit(solution)/shard_map/ppermute | solution.py:225
  58.2 3.3 %collective-permute-start.3 = (bf16[3,4,16,256]{3,2,1,0:T(8,128)(2,1)S(1)}, bf16[3,4,16,256]{3,2,1,0:T(8,128)(2,1)S(1)}, u32[]{:S(2)}, u32[]{:S(2)}) collective-permute-start(bf16[3,4,16,256]{3,2,1,0:T(8,128)(2,1)S(1)} %get-tuple-element.20), channel_id=1, source_target_pairs={{0,6},{2,0},{4,2},{6,4},{1,7},{3,1},{5,3},{7,5},{8,14},{10,8},{12,... | collective-permute-start | bytes 294920 | tf_op jit(solution)/shard_map/ppermute | solution.py:225
  61.5 0.0 collective-permute-done.1.rest_0_
  61.5 0.0 collective-permute-done.2.rest_1_
  61.5 3.1 %collective-permute-done.3.rest_2_ = bf16[3,4,16,256]{3,2,1,0:T(8,128)(2,1)S(1)} collective-permute-done((bf16[3,4,16,256]{3,2,1,0:T(8,128)(2,1)S(1)}, bf16[3,4,16,256]{3,2,1,0:T(8,128)(2,1)S(1)}, u32[]{:S(2)}, u32[]{:S(2)}) %collective-permute-start.3) | collective-permute-done | bytes 98336 | tf_op jit(solution)/shard_map/ppermute | solution.py:225
  64.7 0.0 copy-done.1
  64.7 1.2 %shard_map.68.after_ref.near_ref = f32[4,16,256]{2,1,0:T(8,128)S(1)} custom-call(s32[2,16]{1,0:T(2,128)S(1)} %bitcast.6, bf16[16,1024]{1,0:T(8,128)(2,1)S(1)} %copy-done.4, bf16[5,4,16,256]{3,2,1,0:T(8,128)(2,1)S(1)} %collective-permute-done.got_ref.mate_ref, f32[4,16,256]{2,1,0:T(8,128)S(1)} %get-tuple-element.17.home_ref, ...), custom_call_target="tpu_custom_call" | custom-call | flops 500000000 | bytes 2500000 | tf_op jit(solution)/shard_map/pallas_call | solution.py:269
  65.9 8.0 %all-to-all-done.1.x_ref.back_ref = bf16[8,2,4,16,256]{4,3,2,1,0:T(8,128)(2,1)S(1)} async-done(((bf16[8,2,4,16,256]{4,3,2,1,0:T(8,128)(2,1)}), bf16[8,2,4,16,256]{4,3,2,1,0:T(8,128)(2,1)S(1)}, u32[]{:S(2)}, u32[]{:S(2)}) %all-to-all-start.1) | async-done | bytes 524320 | tf_op jit(solution)/shard_map/all_to_all | solution.py:280
  73.9 0.5 shard_map.69
  74.4 0.0 copy-start.2
  74.4 0.0 copy-start.3
  74.4 0.0 copy-start.6
  74.4 0.0 copy-start.7
  74.4 18.4 %all_to_all.16 = bf16[8,16,16,256]{3,2,1,0:T(8,128)(2,1)S(1)} all-to-all(bf16[8,16,16,256]{3,2,1,0:T(8,128)(2,1)S(1)} %shard_map.69), channel_id=1, replica_groups=mesh['y'=4,'zh'=8,'zl'=2,'x'=4,'c'=2] {'y','zl'}, dimensions={0} | all-to-all | bytes 2097152 | tf_op jit(solution)/shard_map/all_to_all | solution.py:288
  92.9 0.0 copy-done.2
  92.9 0.0 copy-done.3
  92.9 0.0 copy-done.6
  92.9 0.0 copy-done.7
  92.9 2.3 %shard_map.70 = bf16[16,1024]{1,0:T(8,128)(2,1)} custom-call(s32[2,64]{1,0:T(2,128)S(1)} %bitcast.8, s32[64]{0:T(128)S(1)} %copy-done.7, bf16[128,16,256]{2,1,0:T(8,128)(2,1)S(1)} %bitcast.4, bf16[64,32,256]{2,1,0:T(8,128)(2,1)S(1)} %copy-done.2, bf16[64,32,256]{2,1,0:T(8,128)(2,1)S(1)} %copy-done.3, f32[4,16,256]{2,1,0:T(8,128)S(1)} %shard_map.68.after_ref.near_ref, ...), custom_call_target="tpu_custom_call" | custom-call | flops 1000000000 | bytes 3500000 | tf_op jit(solution)/shard_map/pallas_call | solution.py:289
  (1 shorter events, 0.0 us)
Async XLA Ops:
  6.3 22.5 %copy-start.4 = (bf16[16,1024]{1,0:T(8,128)(2,1)S(1)}, bf16[16,1024]{1,0:T(8,128)(2,1)}, u32[]{:S(2)}) copy-start(bf16[16,1024]{1,0:T(8,128)(2,1)} %x_ref.7) | copy-start | bytes 98308
  28.7 15.5 %copy-start.5 = (s32[16,2]{0,1:T(2,128)S(1)}, s32[16,2]{0,1:T(2,128)}, u32[]{:S(2)}) copy-start(s32[16,2]{0,1:T(2,128)} %param.7) | copy-start | bytes 388
  30.4 43.5 %all-to-all-start.1 = ((bf16[8,2,4,16,256]{4,3,2,1,0:T(8,128)(2,1)}), bf16[8,2,4,16,256]{4,3,2,1,0:T(8,128)(2,1)S(1)}, u32[]{:S(2)}, u32[]{:S(2)}) async-start(bf16[8,2,4,16,256]{4,3,2,1,0:T(8,128)(2,1)} %shard_map.65), calls=%async_computation.1 | async-start | bytes 1048576 | tf_op jit(solution)/shard_map/all_to_all | solution.py:280
  44.2 1.6 %copy-start = (bf16[16,256,256]{2,1,0:T(8,128)(2,1)S(1)}, bf16[16,256,256]{2,1,0:T(8,128)(2,1)}, u32[]{:S(2)}) copy-start(bf16[16,256,256]{2,1,0:T(8,128)(2,1)} %rest_3_.1) | copy-start | bytes 6291460
  45.8 18.9 %copy-start.1 = (bf16[16,256,256]{2,1,0:T(8,128)(2,1)S(1)}, bf16[16,256,256]{2,1,0:T(8,128)(2,1)}, u32[]{:S(2)}) copy-start(bf16[16,256,256]{2,1,0:T(8,128)(2,1)} %rest_3_.1) | copy-start | bytes 6291460
  46.8 3.3 %collective-permute-start = (bf16[5,4,16,256]{3,2,1,0:T(8,128)(2,1)S(1)}, bf16[5,4,16,256]{3,2,1,0:T(8,128)(2,1)S(1)}, u32[]{:S(2)}, u32[]{:S(2)}) collective-permute-start(bf16[5,4,16,256]{3,2,1,0:T(8,128)(2,1)S(1)} %get-tuple-element.15), channel_id=1, source_target_pairs={{0,1},{1,0},{2,3},{3,2},{4,5},{5,4},{6,7},{7,6},{8,9},{9,8},{10,11... | collective-permute-start | bytes 491528 | tf_op jit(solution)/shard_map/ppermute | solution.py:225
  50.1 11.4 %collective-permute-start.1 = (bf16[3,4,16,256]{3,2,1,0:T(8,128)(2,1)S(1)}, bf16[3,4,16,256]{3,2,1,0:T(8,128)(2,1)S(1)}, u32[]{:S(2)}, u32[]{:S(2)}) collective-permute-start(bf16[3,4,16,256]{3,2,1,0:T(8,128)(2,1)S(1)} %get-tuple-element.18), channel_id=1, source_target_pairs={{0,2},{2,4},{4,6},{6,0},{1,3},{3,5},{5,7},{7,1},{8,10},{10,12},{12... | collective-permute-start | bytes 294920 | tf_op jit(solution)/shard_map/ppermute | solution.py:225
  53.5 8.0 %collective-permute-start.2 = (bf16[3,4,16,256]{3,2,1,0:T(8,128)(2,1)S(1)}, bf16[3,4,16,256]{3,2,1,0:T(8,128)(2,1)S(1)}, u32[]{:S(2)}, u32[]{:S(2)}) collective-permute-start(bf16[3,4,16,256]{3,2,1,0:T(8,128)(2,1)S(1)} %get-tuple-element.19), channel_id=1, source_target_pairs={{0,4},{2,6},{4,0},{6,2},{1,5},{3,7},{5,1},{7,3},{8,12},{10,14},{12... | collective-permute-start | bytes 294920 | tf_op jit(solution)/shard_map/ppermute | solution.py:225
  58.2 6.5 %collective-permute-start.3 = (bf16[3,4,16,256]{3,2,1,0:T(8,128)(2,1)S(1)}, bf16[3,4,16,256]{3,2,1,0:T(8,128)(2,1)S(1)}, u32[]{:S(2)}, u32[]{:S(2)}) collective-permute-start(bf16[3,4,16,256]{3,2,1,0:T(8,128)(2,1)S(1)} %get-tuple-element.20), channel_id=1, source_target_pairs={{0,6},{2,0},{4,2},{6,4},{1,7},{3,1},{5,3},{7,5},{8,14},{10,8},{12,... | collective-permute-start | bytes 294920 | tf_op jit(solution)/shard_map/ppermute | solution.py:225
  74.4 18.5 %copy-start.2 = (bf16[64,32,256]{2,1,0:T(8,128)(2,1)S(1)}, bf16[64,32,256]{2,1,0:T(8,128)(2,1)}, u32[]{:S(2)}) copy-start(bf16[64,32,256]{2,1,0:T(8,128)(2,1)} %left_ref.1) | copy-start | bytes 3145732
  74.4 18.5 %copy-start.3 = (bf16[64,32,256]{2,1,0:T(8,128)(2,1)S(1)}, bf16[64,32,256]{2,1,0:T(8,128)(2,1)}, u32[]{:S(2)}) copy-start(bf16[64,32,256]{2,1,0:T(8,128)(2,1)} %right_ref.1) | copy-start | bytes 3145732
  74.4 18.5 %copy-start.6 = (s32[64,2]{0,1:T(2,128)S(1)}, s32[64,2]{0,1:T(2,128)}, u32[]{:S(2)}) copy-start(s32[64,2]{0,1:T(2,128)} %param.9) | copy-start | bytes 1540
  74.4 18.4 %copy-start.7 = (s32[64]{0:T(128)S(1)}, s32[64]{0:T(128)}, u32[]{:S(2)}) copy-start(s32[64]{0:T(128)} %get-tuple-element.13.slot_ref) | copy-start | bytes 772

commit v3 on v2

--- a/solution.py
+++ b/solution.py
@@ -9,6 +9,7 @@
 RHS = 16
 PANELS = 256
 RANK = 32
+LANES = 128
 CAP = 2
 CL = 4
 NY = 4
@@ -59,47 +60,45 @@
     return row == col
 
 
+def slot_of(source, count):
+    owner = source // (GRP * CL)
+    order = count[owner]
+    count[owner] = order + 1
+    y = owner // (NZH * NZL)
+    zh = (owner // NZL) % NZH
+    zl = owner % NZL
+    peer = y * NZL + zl
+    return peer, zh * CAP + order
+
+
 def far_send_kernel(
-    far_ref, x_hbm, left_hbm, right_hbm, out_hbm, slot_out,
-    count, table, x_ref, left_ref, right_ref, out_ref, sems,
+    far_hbm, x_hbm, left_hbm, right_hbm, out_ref,
+    far_ref, count, table, x_ref, left_ref, right_ref, sems,
 ):
     loads = [
-        pltpu.make_async_copy(x_hbm, x_ref, sems.at[0]),
-        pltpu.make_async_copy(left_hbm, left_ref, sems.at[1]),
-        pltpu.make_async_copy(right_hbm, right_ref, sems.at[2]),
+        pltpu.make_async_copy(far_hbm, far_ref, sems.at[0]),
+        pltpu.make_async_copy(x_hbm, x_ref, sems.at[1]),
+        pltpu.make_async_copy(left_hbm, left_ref, sems.at[2]),
+        pltpu.make_async_copy(right_hbm, right_ref, sems.at[3]),
     ]
     for load in loads:
         load.start()
-
-    def clear(o, _):
+    for o in range(NY * NZH * NZL):
         count[o] = 0
-        return 0
-
-    lax.fori_loop(0, NY * NZH * NZL, clear, 0)
     table[...] = jnp.zeros(table.shape, F32)
     out_ref[...] = jnp.zeros(out_ref.shape, BF16)
-
-    def place(n, _):
-        source = far_ref[1, n]
-        owner = source // (GRP * CL)
-        order = count[owner]
-        count[owner] = order + 1
-        y = owner // (NZH * NZL)
-        zh = (owner // NZL) % NZH
-        zl = owner % NZL
-        peer = y * NZL + zl
-        within = zh * CAP + order
-        slot_out[n] = peer * (SLOTS + 1) + within
-        table[pl.ds(peer * SLOTS + within, 1), :] = jnp.full((1, PANELS), (source % CL).astype(F32))
-        return 0
-
-    lax.fori_loop(0, FAR, place, 0)
-    for m in range(PEERS):
-        out_ref[m * (SLOTS + 1) + SLOTS] = table[m * SLOTS:(m + 1) * SLOTS, :].astype(BF16)
+    mask = diagonal_mask()
     for load in loads:
         load.wait()
-    mask = diagonal_mask()
     for g in range(GROUPS):
+        slots = []
+        for i in range(BATCH):
+            source = far_ref[1, g * BATCH + i]
+            peer, within = slot_of(source, count)
+            slots.append(peer * (SLOTS + 1) + within)
+            table[pl.ds(peer * SLOTS + within, 1), :] = jnp.full(
+                (1, PANELS), (source % CL).astype(F32)
+            )
         targets = [far_ref[0, g * BATCH + i] % CL for i in range(BATCH)]
         xt = jnp.concatenate(
             [x_ref[:, pl.ds(pl.multiple_of(t * PANELS, PANELS), PANELS)] for t in targets], axis=0
@@ -109,13 +108,20 @@
         coef = jnp.where(mask, dot_nt(xt, left), 0.0).astype(BF16)
         term = dot_nn(coef, right).astype(BF16)
         for i in range(BATCH):
-            out_ref[slot_out[g * BATCH + i]] = term[i * RHS:(i + 1) * RHS, :]
-    store = pltpu.make_async_copy(out_ref, out_hbm, sems.at[3])
-    store.start()
-    store.wait()
-
-
-def near_send_kernel(near_ref, x_ref, blocks_ref, swap_out, own_out, near_sum):
+            out_ref[slots[i]] = term[i * RHS:(i + 1) * RHS, :]
+    for m in range(PEERS):
+        out_ref[m * (SLOTS + 1) + SLOTS] = table[m * SLOTS:(m + 1) * SLOTS, :].astype(BF16)
+
+
+def near_send_kernel(
+    near_ref, far_ref, x_ref, blocks_ref, swap_out, own_out, slot_out, near_sum, count
+):
+    for o in range(NY * NZH * NZL):
+        count[o] = 0
+    for n in range(FAR):
+        peer, within = slot_of(far_ref[1, n], count)
+        slot_out[0, n] = peer * SLOTS + within
+        slot_out[1, n] = far_ref[0, n] % CL
     x = lax.axis_index("x")
     c = lax.axis_index("c")
     for w in range(CL):
@@ -146,31 +152,44 @@
         table = table_ref[m, SLOTS].astype(F32)
         for s in range(SLOTS):
             want = jnp.broadcast_to(table[s:s + 1, :], (RHS, PANELS))
-            block = x_ref[s // CAP, 0, 0].astype(F32)
+            block = x_ref[z_place(s // CAP), 0, 0].astype(F32)
             for w in range(1, CL):
-                block = jnp.where(want == w, x_ref[s // CAP, 0, w].astype(F32), block)
+                block = jnp.where(want == w, x_ref[z_place(s // CAP), 0, w].astype(F32), block)
             out_ref[m, s] = block.astype(BF16)
         return 0
 
     lax.fori_loop(0, PEERS, peer, 0)
 
 
-def merge_kernel(x_ref, in_ref, out_ref):
+def z_place(zh):
+    return NZH - 1 - zh
+
+
+def merge_kernel(x_ref, in_ref, out_hbm, out_ref, table, sems):
     for w in range(CL):
         block = x_ref[:, w * PANELS:(w + 1) * PANELS]
         for zh in range(NZH):
             out_ref[zh, 0, w] = block
-    tables = [in_ref[m, SLOTS].astype(F32) for m in range(PEERS)]
+    for m in range(PEERS):
+        table[m] = in_ref[m, SLOTS][:, :LANES].astype(F32)
+    stores = []
     for zh in range(NZH):
-        sums = [jnp.zeros((RHS, PANELS), F32) for _ in range(CL)]
-        for m in range(PEERS):
-            for s in range(zh * CAP, (zh + 1) * CAP):
-                block = in_ref[m, s].astype(F32)
-                want = jnp.broadcast_to(tables[m][s:s + 1, :], (RHS, PANELS))
-                for w in range(CL):
-                    sums[w] = sums[w] + jnp.where(want == w, block, 0.0)
-        for w in range(CL):
-            out_ref[zh, 1, w] = sums[w].astype(BF16)
+        at = z_place(zh)
+        for h in range(PANELS // LANES):
+            lanes = slice(h * LANES, (h + 1) * LANES)
+            sums = [jnp.zeros((2, RHS // 2, LANES), F32) for _ in range(CL)]
+            for m in range(PEERS):
+                for s in range(zh * CAP, (zh + 1) * CAP):
+                    block = in_ref[m, s, :, lanes].astype(F32).reshape(2, RHS // 2, LANES)
+                    want = jnp.broadcast_to(table[m, s:s + 1, :], (RHS // 2, LANES))
+                    for w in range(CL):
+                        sums[w] = sums[w] + jnp.where((want == w)[None], block, 0.0)
+            for w in range(CL):
+                out_ref[at, 1, w, :, lanes] = sums[w].reshape(RHS, LANES).astype(BF16)
+        stores.append(pltpu.make_async_copy(out_ref.at[at], out_hbm.at[at], sems.at[at]))
+        stores[-1].start()
+    for store in stores:
+        store.wait()
 
 
 def near_kernel(near_ref, x_ref, mate_ref, home_ref, *rest):
@@ -195,7 +214,7 @@
 
 
 def far_kernel(
-    far_ref, slot_ref, x_ref, left_ref, right_ref, near_ref, back_ref, out_ref, spread
+    slot_ref, x_ref, left_ref, right_ref, near_ref, back_ref, out_ref, spread
 ):
     mask = diagonal_mask()
     total = near_ref[...]
@@ -204,14 +223,12 @@
     total = total.reshape(CL * RHS, PANELS)
     spread[...] = jnp.zeros(spread.shape, F32)
     for g in range(GROUPS):
-        slots = [slot_ref[g * BATCH + i] for i in range(BATCH)]
-        xs = jnp.concatenate([x_ref[s - s // (SLOTS + 1)] for s in slots], axis=0)
+        xs = jnp.concatenate([x_ref[slot_ref[0, g * BATCH + i]] for i in range(BATCH)], axis=0)
         left = left_ref[g * BATCH:(g + 1) * BATCH].reshape(BATCH * RANK, PANELS)
         right = right_ref[g * BATCH:(g + 1) * BATCH].reshape(BATCH * RANK, PANELS)
         coef = jnp.where(mask, dot_nt(xs, right), 0.0)
         for i in range(BATCH):
-            target = far_ref[0, g * BATCH + i] % CL
-            spread[g, target] += coef[i * RHS:(i + 1) * RHS, :]
+            spread[g, slot_ref[1, g * BATCH + i]] += coef[i * RHS:(i + 1) * RHS, :]
         total = total + dot_nn(spread[g].reshape(CL * RHS, PANELS).astype(BF16), left)
     for w in range(CL):
         out_ref[:, w * PANELS:(w + 1) * PANELS] = total[w * RHS:(w + 1) * RHS].astype(BF16)
@@ -229,34 +246,37 @@
     near_table = near_pairs.T
     far_table = far_pairs.T
     block = (CL, RHS, PANELS)
-    far_send, slots = call(
+    far_send = call(
         far_send_kernel,
-        (shape((PEERS * (SLOTS + 1), RHS, PANELS)), shape((FAR,), jnp.int32)),
-        [SMEM, ANY, ANY, ANY],
-        (ANY, SMEM),
+        shape((PEERS * (SLOTS + 1), RHS, PANELS)),
+        [ANY] * 4,
+        VMEM,
         [
+            pltpu.SMEM(far_table.shape, jnp.int32),
             pltpu.SMEM((NY * NZH * NZL,), jnp.int32),
             pltpu.VMEM((PEERS * SLOTS, PANELS), F32),
             pltpu.VMEM(sources.shape, BF16),
             pltpu.VMEM(far_left.shape, BF16),
             pltpu.VMEM(far_right.shape, BF16),
-            pltpu.VMEM((PEERS * (SLOTS + 1), RHS, PANELS), BF16),
             pltpu.SemaphoreType.DMA((4,)),
         ],
         cost=(1000000000, 3500000),
-        vmem=60,
+        vmem=58,
     )(far_table, sources, far_left, far_right)
     far_got = lax.all_to_all(
-        far_send.reshape(PEERS, SLOTS + 1, RHS, PANELS), ("y", "zl"), 0, 0, tiled=True
-    )
-    swap, own = call(
+        far_send.reshape(PEERS, SLOTS + 1, RHS, PANELS), ("y", "e"), 0, 0, tiled=True
+    )
+    swap, own, slots = call(
         near_send_kernel,
-        (shape((1 + NX, *block)), shape((NX, *block), F32)),
-        [SMEM, VMEM, VMEM],
-        (VMEM, VMEM),
-        [pltpu.VMEM((GRP * CL, RHS, PANELS), F32)],
+        (shape((1 + NX, *block)), shape((NX, *block), F32), shape((2, FAR), jnp.int32)),
+        [SMEM, SMEM, VMEM, VMEM],
+        (VMEM, VMEM, SMEM),
+        [
+            pltpu.VMEM((GRP * CL, RHS, PANELS), F32),
+            pltpu.SMEM((NY * NZH * NZL,), jnp.int32),
+        ],
         cost=(1000000000, 3500000),
-    )(near_table, sources, near_blocks)
+    )(near_table, far_table, sources, near_blocks)
     mate = shift(swap, "c", NC, 1)
     home, *packs = call(
         near_pack_kernel,
@@ -275,9 +295,20 @@
         cost=(500000000, 2500000),
     )(near_table, sources, mate, home, *got, near_blocks)
     merged = call(
-        merge_kernel, shape((NZH, 2, *block)), [VMEM, VMEM], WHOLE, cost=(0, 2000000)
+        merge_kernel,
+        shape((NZH, 2, *block)),
+        [VMEM, VMEM],
+        ANY,
+        [
+            pltpu.VMEM((NZH, 2, *block), BF16),
+            pltpu.VMEM((PEERS, SLOTS, LANES), F32),
+            pltpu.SemaphoreType.DMA((NZH,)),
+        ],
+        cost=(0, 2000000),
     )(sources, far_got)
-    along_z = lax.all_to_all(merged, "zh", 0, 0, tiled=True)
+    along_z = lax.all_to_all(
+        merged, "zh", 0, 0, axis_index_groups=[list(range(NZH))[::-1]], tiled=True
+    )
     picked = call(
         pick_kernel,
         shape((PEERS, SLOTS, RHS, PANELS)),
@@ -285,22 +316,22 @@
         WHOLE,
         cost=(0, 2000000),
     )(along_z, far_got, near_total)
-    far_sources = lax.all_to_all(picked, ("y", "zl"), 0, 0, tiled=True)
+    far_sources = lax.all_to_all(picked, ("y", "e"), 0, 0, tiled=True)
     return call(
         far_kernel,
         shape(sources.shape),
-        [SMEM, SMEM] + [VMEM] * 5,
+        [SMEM] + [VMEM] * 5,
         VMEM,
         [pltpu.VMEM((GROUPS, *block), F32)],
         cost=(1000000000, 3500000),
     )(
-        far_table, slots, far_sources.reshape(PEERS * SLOTS, RHS, PANELS),
+        slots, far_sources.reshape(PEERS * SLOTS, RHS, PANELS),
         far_left, far_right, near_total, along_z,
     )
 
 
 def solution(mesh):
-    axes = ("y", "zh", "zl", "x", "c")
+    axes = ("y", "zh", "e", "x", "c")
     fine = Mesh(mesh.devices.reshape(NY, NZH, NZL, NX, NC), axes)
     placed = (
         P(None, axes),

time: 95.6 us -> 89.6 us (0.937)
  the two profiles are of different devices: /device:TPU:64 before, /device:TPU:68 now
where the time goes in v3:
time: 89.6 us; the launch traced here: 89.1 us
  blocking collectives  41.1 us (46%)
  starting transfers between devices  24.6 us (27%)
  Pallas kernels  13 us (15%)
  waiting for transfers between devices  8.64 us (10%)
  local copies, waits for them, and re-layouts  1.62 us (2%)
    all_to_all x1, blocking collectives, on_device(): lax.all_to_all(far_send.reshape(PEERS, SLOTS + 1, RHS, PANELS), ('y', 'e'...  22.4 us
    all_to_all x1, blocking collectives, on_device(): far_sources = lax.all_to_all(picked, ('y', 'e'), 0, 0, tiled=True)  18.6 us
    all_to_all x1, starting transfers between devices, on_device(): lax.all_to_all(merged, 'zh', 0, 0, axis_index_groups=[list(range(NZH))[::...  13.9 us
    ppermute x4, starting transfers between devices, shift(): lax.ppermute(array, axis, [(i, (i + by) % size) for i in range(size)])  10.8 us
    ppermute x4, waiting for transfers between devices, shift(): lax.ppermute(array, axis, [(i, (i + by) % size) for i in range(size)])  5.06 us
    pallas_call x1, Pallas kernels, on_device(): call(far_send_kernel, shape((PEERS * (SLOTS + 1), RHS, PANELS)), [ANY] *...  4.67 us
    all_to_all x1, waiting for transfers between devices, on_device(): lax.all_to_all(merged, 'zh', 0, 0, axis_index_groups=[list(range(NZH))[::...  3.57 us
    pallas_call x1, Pallas kernels, on_device(): call(near_send_kernel, (shape((1 + NX, *block)), shape((NX, *block), F32)...  2.75 us
  transfers between devices with their start and end apart: 5, of which 4 were waited for; matrix products, arithmetic and copies ran while one was open for 0% of the time, Pallas kernels for 4%

profile of v3, /device:TPU:68, one launch (start us, length us, event | category | flops | bytes accessed | tf_op | source)
XLA Modules:
  0.0 89.1 jit_solution(11858442074084826811)
XLA Ops:
  0.0 4.7 %shard_map.65 = bf16[136,16,256]{2,1,0:T(8,128)(2,1)} custom-call(s32[2,64]{1,0:T(2,128)} %bitcast.7, bf16[16,1024]{1,0:T(8,128)(2,1)} %x_ref.7, bf16[64,32,256]{2,1,0:T(8,128)(2,1)} %left_ref.1, bf16[64,32,256]{2,1,0:T(8,128)(2,1)} %right_ref.1), custom_call_target="tpu_custom_call" | custom-call | flops 1000000000 | bytes 3500000 | tf_op jit(solution)/shard_map/pallas_call | solution.py:249
  4.7 0.0 copy-start.4
  4.7 22.4 %all_to_all.15.in_ref.table_ref = bf16[8,17,16,256]{3,2,1,0:T(8,128)(2,1)S(1)} all-to-all(bf16[8,17,16,256]{3,2,1,0:T(8,128)(2,1)} %bitcast.9), channel_id=1, replica_groups=mesh['y'=4,'zh'=8,'e'=2,'x'=4,'c'=2] {'y','e'}, dimensions={0} | all-to-all | bytes 2228224 | tf_op jit(solution)/shard_map/all_to_all | solution.py:266
  27.1 0.0 copy-done.4
  27.1 0.0 copy-start.5
  27.1 0.0 copy-start.6
  27.1 1.5 %shard_map.66 = bf16[8,2,4,16,256]{4,3,2,1,0:T(8,128)(2,1)} custom-call(bf16[16,1024]{1,0:T(8,128)(2,1)S(1)} %copy-done.4, bf16[8,17,16,256]{3,2,1,0:T(8,128)(2,1)S(1)} %all_to_all.15.in_ref.table_ref), custom_call_target="tpu_custom_call" | custom-call | bytes 2000000 | tf_op jit(solution)/shard_map/pallas_call | solution.py:297
  28.7 13.9 %all-to-all-start.1 = ((bf16[8,2,4,16,256]{4,3,2,1,0:T(8,128)(2,1)}), bf16[8,2,4,16,256]{4,3,2,1,0:T(8,128)(2,1)S(1)}, u32[]{:S(2)}, u32[]{:S(2)}) async-start(bf16[8,2,4,16,256]{4,3,2,1,0:T(8,128)(2,1)} %shard_map.66), calls=%async_computation.1 | async-start | bytes 1048576 | tf_op jit(solution)/shard_map/all_to_all | solution.py:309
  42.5 0.0 copy-done.5
  42.5 0.0 copy-done.6
  42.5 0.0 copy-start
  42.6 1.6 %copy-done = bf16[16,256,256]{2,1,0:T(8,128)(2,1)S(1)} copy-done((bf16[16,256,256]{2,1,0:T(8,128)(2,1)S(1)}, bf16[16,256,256]{2,1,0:T(8,128)(2,1)}, u32[]{:S(2)}) %copy-start) | copy-done | bytes 2097176
  44.1 0.0 copy-start.1
  44.1 2.7 %shard_map.64 = (bf16[5,4,16,256]{3,2,1,0:T(8,128)(2,1)S(1)}, f32[4,4,16,256]{3,2,1,0:T(8,128)S(1)}, s32[2,64]{1,0:T(2,128)S(1)}) custom-call(s32[2,16]{1,0:T(2,128)S(1)} %bitcast.5, s32[2,64]{1,0:T(2,128)S(1)} %bitcast.8, bf16[16,1024]{1,0:T(8,128)(2,1)S(1)} %copy-done.4, bf16[16,256,256]{2,1,0:T(8,128)(2,1)S(1)} %copy-done), custom_call_target="tpu_custom_call" | custom-call | flops 1000000000 | bytes 3500000 | tf_op jit(solution)/shard_map/pallas_call | solution.py:269
  46.9 1.9 %collective-permute-start = (bf16[5,4,16,256]{3,2,1,0:T(8,128)(2,1)S(1)}, bf16[5,4,16,256]{3,2,1,0:T(8,128)(2,1)S(1)}, u32[]{:S(2)}, u32[]{:S(2)}) collective-permute-start(bf16[5,4,16,256]{3,2,1,0:T(8,128)(2,1)S(1)} %get-tuple-element.13), channel_id=1, source_target_pairs={{0,1},{1,0},{2,3},{3,2},{4,5},{5,4},{6,7},{7,6},{8,9},{9,8},{10,11... | collective-permute-start | bytes 491528 | tf_op jit(solution)/shard_map/ppermute | solution.py:242
  48.8 1.4 %collective-permute-done.got_ref.mate_ref = bf16[5,4,16,256]{3,2,1,0:T(8,128)(2,1)S(1)} collective-permute-done((bf16[5,4,16,256]{3,2,1,0:T(8,128)(2,1)S(1)}, bf16[5,4,16,256]{3,2,1,0:T(8,128)(2,1)S(1)}, u32[]{:S(2)}, u32[]{:S(2)}) %collective-permute-start) | collective-permute-done | bytes 163872 | tf_op jit(solution)/shard_map/ppermute | solution.py:242
  50.2 3.1 %collective-permute-start.1 = (bf16[3,4,16,256]{3,2,1,0:T(8,128)(2,1)S(1)}, bf16[3,4,16,256]{3,2,1,0:T(8,128)(2,1)S(1)}, u32[]{:S(2)}, u32[]{:S(2)}) collective-permute-start(bf16[3,4,16,256]{3,2,1,0:T(8,128)(2,1)S(1)} %get-tuple-element.16), channel_id=1, source_target_pairs={{0,2},{2,4},{4,6},{6,0},{1,3},{3,5},{5,7},{7,1},{8,10},{10,12},{12... | collective-permute-start | bytes 294920 | tf_op jit(solution)/shard_map/ppermute | solution.py:242
  53.3 2.7 %collective-permute-start.2 = (bf16[3,4,16,256]{3,2,1,0:T(8,128)(2,1)S(1)}, bf16[3,4,16,256]{3,2,1,0:T(8,128)(2,1)S(1)}, u32[]{:S(2)}, u32[]{:S(2)}) collective-permute-start(bf16[3,4,16,256]{3,2,1,0:T(8,128)(2,1)S(1)} %get-tuple-element.17), channel_id=1, source_target_pairs={{0,4},{2,6},{4,0},{6,2},{1,5},{3,7},{5,1},{7,3},{8,12},{10,14},{12... | collective-permute-start | bytes 294920 | tf_op jit(solution)/shard_map/ppermute | solution.py:242
  56.1 3.0 %collective-permute-start.3 = (bf16[3,4,16,256]{3,2,1,0:T(8,128)(2,1)S(1)}, bf16[3,4,16,256]{3,2,1,0:T(8,128)(2,1)S(1)}, u32[]{:S(2)}, u32[]{:S(2)}) collective-permute-start(bf16[3,4,16,256]{3,2,1,0:T(8,128)(2,1)S(1)} %get-tuple-element.18), channel_id=1, source_target_pairs={{0,6},{2,0},{4,2},{6,4},{1,7},{3,1},{5,3},{7,5},{8,14},{10,8},{12,... | collective-permute-start | bytes 294920 | tf_op jit(solution)/shard_map/ppermute | solution.py:242
  59.1 0.0 collective-permute-done.1.rest_0_
  59.1 2.2 %collective-permute-done.2.rest_1_ = bf16[3,4,16,256]{3,2,1,0:T(8,128)(2,1)S(1)} collective-permute-done((bf16[3,4,16,256]{3,2,1,0:T(8,128)(2,1)S(1)}, bf16[3,4,16,256]{3,2,1,0:T(8,128)(2,1)S(1)}, u32[]{:S(2)}, u32[]{:S(2)}) %collective-permute-start.2) | collective-permute-done | bytes 98336 | tf_op jit(solution)/shard_map/ppermute | solution.py:242
  61.4 1.5 %collective-permute-done.3.rest_2_ = bf16[3,4,16,256]{3,2,1,0:T(8,128)(2,1)S(1)} collective-permute-done((bf16[3,4,16,256]{3,2,1,0:T(8,128)(2,1)S(1)}, bf16[3,4,16,256]{3,2,1,0:T(8,128)(2,1)S(1)}, u32[]{:S(2)}, u32[]{:S(2)}) %collective-permute-start.3) | collective-permute-done | bytes 98336 | tf_op jit(solution)/shard_map/ppermute | solution.py:242
  62.8 0.0 copy-done.1
  62.8 1.2 %shard_map.68.after_ref.near_ref = f32[4,16,256]{2,1,0:T(8,128)S(1)} custom-call(s32[2,16]{1,0:T(2,128)S(1)} %bitcast.6, bf16[16,1024]{1,0:T(8,128)(2,1)S(1)} %copy-done.4, bf16[5,4,16,256]{3,2,1,0:T(8,128)(2,1)S(1)} %collective-permute-done.got_ref.mate_ref, f32[4,16,256]{2,1,0:T(8,128)S(1)} %get-tuple-element.15.home_ref, ...), custom_call_target="tpu_custom_call" | custom-call | flops 500000000 | bytes 2500000 | tf_op jit(solution)/shard_map/pallas_call | solution.py:289
  64.0 3.6 %all-to-all-done.1.x_ref.back_ref = bf16[8,2,4,16,256]{4,3,2,1,0:T(8,128)(2,1)S(1)} async-done(((bf16[8,2,4,16,256]{4,3,2,1,0:T(8,128)(2,1)}), bf16[8,2,4,16,256]{4,3,2,1,0:T(8,128)(2,1)S(1)}, u32[]{:S(2)}, u32[]{:S(2)}) %all-to-all-start.1) | async-done | bytes 524320 | tf_op jit(solution)/shard_map/all_to_all | solution.py:309
  67.6 0.5 shard_map.69
  68.1 0.0 copy-start.2
  68.2 0.0 copy-start.3
  68.2 18.6 %all_to_all.16 = bf16[8,16,16,256]{3,2,1,0:T(8,128)(2,1)S(1)} all-to-all(bf16[8,16,16,256]{3,2,1,0:T(8,128)(2,1)S(1)} %shard_map.69), channel_id=1, replica_groups=mesh['y'=4,'zh'=8,'e'=2,'x'=4,'c'=2] {'y','e'}, dimensions={0} | all-to-all | bytes 2097152 | tf_op jit(solution)/shard_map/all_to_all | solution.py:319
  86.8 0.0 copy-done.2
  86.8 0.0 copy-done.3
  86.8 2.3 %shard_map.70 = bf16[16,1024]{1,0:T(8,128)(2,1)} custom-call(s32[2,64]{1,0:T(2,128)S(1)} %get-tuple-element.12.slot_ref, bf16[128,16,256]{2,1,0:T(8,128)(2,1)S(1)} %bitcast.4, bf16[64,32,256]{2,1,0:T(8,128)(2,1)S(1)} %copy-done.2, bf16[64,32,256]{2,1,0:T(8,128)(2,1)S(1)} %copy-done.3, f32[4,16,256]{2,1,0:T(8,128)S(1)} %shard_map.68.after_ref.near_ref, ...), custom_call_target="tpu_custom_call" | custom-call | flops 1000000000 | bytes 3500000 | tf_op jit(solution)/shard_map/pallas_call | solution.py:320
  (1 shorter events, 0.0 us)
Async XLA Ops:
  4.7 22.4 %copy-start.4 = (bf16[16,1024]{1,0:T(8,128)(2,1)S(1)}, bf16[16,1024]{1,0:T(8,128)(2,1)}, u32[]{:S(2)}) copy-start(bf16[16,1024]{1,0:T(8,128)(2,1)} %x_ref.7) | copy-start | bytes 98308
  27.1 15.4 %copy-start.5 = (s32[16,2]{0,1:T(2,128)S(1)}, s32[16,2]{0,1:T(2,128)}, u32[]{:S(2)}) copy-start(s32[16,2]{0,1:T(2,128)} %param.7) | copy-start | bytes 388
  27.1 15.4 %copy-start.6 = (s32[64,2]{0,1:T(2,128)S(1)}, s32[64,2]{0,1:T(2,128)}, u32[]{:S(2)}) copy-start(s32[64,2]{0,1:T(2,128)} %param.9) | copy-start | bytes 1540
  28.7 38.9 %all-to-all-start.1 = ((bf16[8,2,4,16,256]{4,3,2,1,0:T(8,128)(2,1)}), bf16[8,2,4,16,256]{4,3,2,1,0:T(8,128)(2,1)S(1)}, u32[]{:S(2)}, u32[]{:S(2)}) async-start(bf16[8,2,4,16,256]{4,3,2,1,0:T(8,128)(2,1)} %shard_map.66), calls=%async_computation.1 | async-start | bytes 1048576 | tf_op jit(solution)/shard_map/all_to_all | solution.py:309
  42.5 1.6 %copy-start = (bf16[16,256,256]{2,1,0:T(8,128)(2,1)S(1)}, bf16[16,256,256]{2,1,0:T(8,128)(2,1)}, u32[]{:S(2)}) copy-start(bf16[16,256,256]{2,1,0:T(8,128)(2,1)} %rest_3_.1) | copy-start | bytes 6291460
  44.1 18.7 %copy-start.1 = (bf16[16,256,256]{2,1,0:T(8,128)(2,1)S(1)}, bf16[16,256,256]{2,1,0:T(8,128)(2,1)}, u32[]{:S(2)}) copy-start(bf16[16,256,256]{2,1,0:T(8,128)(2,1)} %rest_3_.1) | copy-start | bytes 6291460
  46.9 3.3 %collective-permute-start = (bf16[5,4,16,256]{3,2,1,0:T(8,128)(2,1)S(1)}, bf16[5,4,16,256]{3,2,1,0:T(8,128)(2,1)S(1)}, u32[]{:S(2)}, u32[]{:S(2)}) collective-permute-start(bf16[5,4,16,256]{3,2,1,0:T(8,128)(2,1)S(1)} %get-tuple-element.13), channel_id=1, source_target_pairs={{0,1},{1,0},{2,3},{3,2},{4,5},{5,4},{6,7},{7,6},{8,9},{9,8},{10,11... | collective-permute-start | bytes 491528 | tf_op jit(solution)/shard_map/ppermute | solution.py:242
  50.2 8.9 %collective-permute-start.1 = (bf16[3,4,16,256]{3,2,1,0:T(8,128)(2,1)S(1)}, bf16[3,4,16,256]{3,2,1,0:T(8,128)(2,1)S(1)}, u32[]{:S(2)}, u32[]{:S(2)}) collective-permute-start(bf16[3,4,16,256]{3,2,1,0:T(8,128)(2,1)S(1)} %get-tuple-element.16), channel_id=1, source_target_pairs={{0,2},{2,4},{4,6},{6,0},{1,3},{3,5},{5,7},{7,1},{8,10},{10,12},{12... | collective-permute-start | bytes 294920 | tf_op jit(solution)/shard_map/ppermute | solution.py:242
  53.3 8.0 %collective-permute-start.2 = (bf16[3,4,16,256]{3,2,1,0:T(8,128)(2,1)S(1)}, bf16[3,4,16,256]{3,2,1,0:T(8,128)(2,1)S(1)}, u32[]{:S(2)}, u32[]{:S(2)}) collective-permute-start(bf16[3,4,16,256]{3,2,1,0:T(8,128)(2,1)S(1)} %get-tuple-element.17), channel_id=1, source_target_pairs={{0,4},{2,6},{4,0},{6,2},{1,5},{3,7},{5,1},{7,3},{8,12},{10,14},{12... | collective-permute-start | bytes 294920 | tf_op jit(solution)/shard_map/ppermute | solution.py:242
  56.1 6.8 %collective-permute-start.3 = (bf16[3,4,16,256]{3,2,1,0:T(8,128)(2,1)S(1)}, bf16[3,4,16,256]{3,2,1,0:T(8,128)(2,1)S(1)}, u32[]{:S(2)}, u32[]{:S(2)}) collective-permute-start(bf16[3,4,16,256]{3,2,1,0:T(8,128)(2,1)S(1)} %get-tuple-element.18), channel_id=1, source_target_pairs={{0,6},{2,0},{4,2},{6,4},{1,7},{3,1},{5,3},{7,5},{8,14},{10,8},{12,... | collective-permute-start | bytes 294920 | tf_op jit(solution)/shard_map/ppermute | solution.py:242
  68.1 18.7 %copy-start.2 = (bf16[64,32,256]{2,1,0:T(8,128)(2,1)S(1)}, bf16[64,32,256]{2,1,0:T(8,128)(2,1)}, u32[]{:S(2)}) copy-start(bf16[64,32,256]{2,1,0:T(8,128)(2,1)} %left_ref.1) | copy-start | bytes 3145732
  68.2 18.7 %copy-start.3 = (bf16[64,32,256]{2,1,0:T(8,128)(2,1)S(1)}, bf16[64,32,256]{2,1,0:T(8,128)(2,1)}, u32[]{:S(2)}) copy-start(bf16[64,32,256]{2,1,0:T(8,128)(2,1)} %right_ref.1) | copy-start | bytes 3145732

commit v4 on v3

--- a/solution.py
+++ b/solution.py
@@ -24,6 +24,7 @@
 FAR = 64
 BATCH = 8
 GROUPS = FAR // BATCH
+PARTS = 4
 ROWS = BATCH * RHS
 F32 = jnp.float32
 BF16 = jnp.bfloat16
@@ -78,9 +79,13 @@
     loads = [
         pltpu.make_async_copy(far_hbm, far_ref, sems.at[0]),
         pltpu.make_async_copy(x_hbm, x_ref, sems.at[1]),
-        pltpu.make_async_copy(left_hbm, left_ref, sems.at[2]),
-        pltpu.make_async_copy(right_hbm, right_ref, sems.at[3]),
     ]
+    for p in range(PARTS):
+        pairs = pl.ds(p * (FAR // PARTS), FAR // PARTS)
+        for i, (hbm, ref) in enumerate(((left_hbm, left_ref), (right_hbm, right_ref))):
+            loads.append(
+                pltpu.make_async_copy(hbm.at[pairs], ref.at[pairs], sems.at[2 + 2 * p + i])
+            )
     for load in loads:
         load.start()
     for o in range(NY * NZH * NZL):
@@ -88,9 +93,13 @@
     table[...] = jnp.zeros(table.shape, F32)
     out_ref[...] = jnp.zeros(out_ref.shape, BF16)
     mask = diagonal_mask()
-    for load in loads:
-        load.wait()
+    loads[0].wait()
+    loads[1].wait()
     for g in range(GROUPS):
+        if g % (GROUPS // PARTS) == 0:
+            part = g // (GROUPS // PARTS)
+            loads[2 + 2 * part].wait()
+            loads[3 + 2 * part].wait()
         slots = []
         for i in range(BATCH):
             source = far_ref[1, g * BATCH + i]
@@ -258,7 +267,7 @@
             pltpu.VMEM(sources.shape, BF16),
             pltpu.VMEM(far_left.shape, BF16),
             pltpu.VMEM(far_right.shape, BF16),
-            pltpu.SemaphoreType.DMA((4,)),
+            pltpu.SemaphoreType.DMA((2 + 2 * PARTS,)),
         ],
         cost=(1000000000, 3500000),
         vmem=58,

time: 89.6 us -> 89.7 us (level)
  the two profiles are of different devices: /device:TPU:68 before, /device:TPU:70 now
where the time goes in v4:
time: 89.7 us; the launch traced here: 89.2 us
  blocking collectives  41.1 us (46%)
  starting transfers between devices  24.4 us (27%)
  Pallas kernels  13.1 us (15%)
  waiting for transfers between devices  8.86 us (10%)
  local copies, waits for them, and re-layouts  1.62 us (2%)
    all_to_all x1, blocking collectives, on_device(): lax.all_to_all(far_send.reshape(PEERS, SLOTS + 1, RHS, PANELS), ('y', 'e'...  22.4 us
    all_to_all x1, blocking collectives, on_device(): far_sources = lax.all_to_all(picked, ('y', 'e'), 0, 0, tiled=True)  18.6 us
    all_to_all x1, starting transfers between devices, on_device(): lax.all_to_all(merged, 'zh', 0, 0, axis_index_groups=[list(range(NZH))[::...  13.9 us
    ppermute x4, starting transfers between devices, shift(): lax.ppermute(array, axis, [(i, (i + by) % size) for i in range(size)])  10.6 us
    ppermute x4, waiting for transfers between devices, shift(): lax.ppermute(array, axis, [(i, (i + by) % size) for i in range(size)])  7.14 us
    pallas_call x1, Pallas kernels, on_device(): call(far_send_kernel, shape((PEERS * (SLOTS + 1), RHS, PANELS)), [ANY] *...  4.78 us
    pallas_call x1, Pallas kernels, on_device(): call(near_send_kernel, (shape((1 + NX, *block)), shape((NX, *block), F32)...  2.75 us
    pallas_call x1, Pallas kernels, on_device(): call(far_kernel, shape(sources.shape), [SMEM] + [VMEM] * 5, VMEM, [pltpu....  2.28 us
  transfers between devices with their start and end apart: 5, of which 4 were waited for; matrix products, arithmetic and copies ran while one was open for 0% of the time, Pallas kernels for 4%

profile of v4, /device:TPU:70, one launch (start us, length us, event | category | flops | bytes accessed | tf_op | source)
XLA Modules:
  0.0 89.2 jit_solution(10252790885177371271)
XLA Ops:
  0.0 4.8 %shard_map.65 = bf16[136,16,256]{2,1,0:T(8,128)(2,1)} custom-call(s32[2,64]{1,0:T(2,128)} %bitcast.7, bf16[16,1024]{1,0:T(8,128)(2,1)} %x_ref.7, bf16[64,32,256]{2,1,0:T(8,128)(2,1)} %left_ref.1, bf16[64,32,256]{2,1,0:T(8,128)(2,1)} %right_ref.1), custom_call_target="tpu_custom_call" | custom-call | flops 1000000000 | bytes 3500000 | tf_op jit(solution)/shard_map/pallas_call | solution.py:258
  4.8 0.0 copy-start.4
  4.8 22.4 %all_to_all.15.in_ref.table_ref = bf16[8,17,16,256]{3,2,1,0:T(8,128)(2,1)S(1)} all-to-all(bf16[8,17,16,256]{3,2,1,0:T(8,128)(2,1)} %bitcast.9), channel_id=1, replica_groups=mesh['y'=4,'zh'=8,'e'=2,'x'=4,'c'=2] {'y','e'}, dimensions={0} | all-to-all | bytes 2228224 | tf_op jit(solution)/shard_map/all_to_all | solution.py:275
  27.2 0.0 copy-done.4
  27.2 0.0 copy-start.5
  27.2 0.0 copy-start.6
  27.2 1.5 %shard_map.66 = bf16[8,2,4,16,256]{4,3,2,1,0:T(8,128)(2,1)} custom-call(bf16[16,1024]{1,0:T(8,128)(2,1)S(1)} %copy-done.4, bf16[8,17,16,256]{3,2,1,0:T(8,128)(2,1)S(1)} %all_to_all.15.in_ref.table_ref), custom_call_target="tpu_custom_call" | custom-call | bytes 2000000 | tf_op jit(solution)/shard_map/pallas_call | solution.py:306
  28.8 13.9 %all-to-all-start.1 = ((bf16[8,2,4,16,256]{4,3,2,1,0:T(8,128)(2,1)}), bf16[8,2,4,16,256]{4,3,2,1,0:T(8,128)(2,1)S(1)}, u32[]{:S(2)}, u32[]{:S(2)}) async-start(bf16[8,2,4,16,256]{4,3,2,1,0:T(8,128)(2,1)} %shard_map.66), calls=%async_computation.1 | async-start | bytes 1048576 | tf_op jit(solution)/shard_map/all_to_all | solution.py:318
  42.6 0.0 copy-done.5
  42.6 0.0 copy-done.6
  42.7 0.0 copy-start
  42.7 1.6 %copy-done = bf16[16,256,256]{2,1,0:T(8,128)(2,1)S(1)} copy-done((bf16[16,256,256]{2,1,0:T(8,128)(2,1)S(1)}, bf16[16,256,256]{2,1,0:T(8,128)(2,1)}, u32[]{:S(2)}) %copy-start) | copy-done | bytes 2097176
  44.2 0.0 copy-start.1
  44.2 2.7 %shard_map.64 = (bf16[5,4,16,256]{3,2,1,0:T(8,128)(2,1)S(1)}, f32[4,4,16,256]{3,2,1,0:T(8,128)S(1)}, s32[2,64]{1,0:T(2,128)S(1)}) custom-call(s32[2,16]{1,0:T(2,128)S(1)} %bitcast.5, s32[2,64]{1,0:T(2,128)S(1)} %bitcast.8, bf16[16,1024]{1,0:T(8,128)(2,1)S(1)} %copy-done.4, bf16[16,256,256]{2,1,0:T(8,128)(2,1)S(1)} %copy-done), custom_call_target="tpu_custom_call" | custom-call | flops 1000000000 | bytes 3500000 | tf_op jit(solution)/shard_map/pallas_call | solution.py:278
  47.0 1.9 %collective-permute-start = (bf16[5,4,16,256]{3,2,1,0:T(8,128)(2,1)S(1)}, bf16[5,4,16,256]{3,2,1,0:T(8,128)(2,1)S(1)}, u32[]{:S(2)}, u32[]{:S(2)}) collective-permute-start(bf16[5,4,16,256]{3,2,1,0:T(8,128)(2,1)S(1)} %get-tuple-element.13), channel_id=1, source_target_pairs={{0,1},{1,0},{2,3},{3,2},{4,5},{5,4},{6,7},{7,6},{8,9},{9,8},{10,11... | collective-permute-start | bytes 491528 | tf_op jit(solution)/shard_map/ppermute | solution.py:251
  48.9 1.4 %collective-permute-done.got_ref.mate_ref = bf16[5,4,16,256]{3,2,1,0:T(8,128)(2,1)S(1)} collective-permute-done((bf16[5,4,16,256]{3,2,1,0:T(8,128)(2,1)S(1)}, bf16[5,4,16,256]{3,2,1,0:T(8,128)(2,1)S(1)}, u32[]{:S(2)}, u32[]{:S(2)}) %collective-permute-start) | collective-permute-done | bytes 163872 | tf_op jit(solution)/shard_map/ppermute | solution.py:251
  50.3 2.4 %collective-permute-start.1 = (bf16[3,4,16,256]{3,2,1,0:T(8,128)(2,1)S(1)}, bf16[3,4,16,256]{3,2,1,0:T(8,128)(2,1)S(1)}, u32[]{:S(2)}, u32[]{:S(2)}) collective-permute-start(bf16[3,4,16,256]{3,2,1,0:T(8,128)(2,1)S(1)} %get-tuple-element.16), channel_id=1, source_target_pairs={{0,2},{2,4},{4,6},{6,0},{1,3},{3,5},{5,7},{7,1},{8,10},{10,12},{12... | collective-permute-start | bytes 294920 | tf_op jit(solution)/shard_map/ppermute | solution.py:251
  52.7 4.3 %collective-permute-start.2 = (bf16[3,4,16,256]{3,2,1,0:T(8,128)(2,1)S(1)}, bf16[3,4,16,256]{3,2,1,0:T(8,128)(2,1)S(1)}, u32[]{:S(2)}, u32[]{:S(2)}) collective-permute-start(bf16[3,4,16,256]{3,2,1,0:T(8,128)(2,1)S(1)} %get-tuple-element.17), channel_id=1, source_target_pairs={{0,4},{2,6},{4,0},{6,2},{1,5},{3,7},{5,1},{7,3},{8,12},{10,14},{12... | collective-permute-start | bytes 294920 | tf_op jit(solution)/shard_map/ppermute | solution.py:251
  57.1 1.9 %collective-permute-start.3 = (bf16[3,4,16,256]{3,2,1,0:T(8,128)(2,1)S(1)}, bf16[3,4,16,256]{3,2,1,0:T(8,128)(2,1)S(1)}, u32[]{:S(2)}, u32[]{:S(2)}) collective-permute-start(bf16[3,4,16,256]{3,2,1,0:T(8,128)(2,1)S(1)} %get-tuple-element.18), channel_id=1, source_target_pairs={{0,6},{2,0},{4,2},{6,4},{1,7},{3,1},{5,3},{7,5},{8,14},{10,8},{12,... | collective-permute-start | bytes 294920 | tf_op jit(solution)/shard_map/ppermute | solution.py:251
  59.0 0.0 collective-permute-done.1.rest_0_
  59.0 1.7 %collective-permute-done.2.rest_1_ = bf16[3,4,16,256]{3,2,1,0:T(8,128)(2,1)S(1)} collective-permute-done((bf16[3,4,16,256]{3,2,1,0:T(8,128)(2,1)S(1)}, bf16[3,4,16,256]{3,2,1,0:T(8,128)(2,1)S(1)}, u32[]{:S(2)}, u32[]{:S(2)}) %collective-permute-start.2) | collective-permute-done | bytes 98336 | tf_op jit(solution)/shard_map/ppermute | solution.py:251
  60.7 4.0 %collective-permute-done.3.rest_2_ = bf16[3,4,16,256]{3,2,1,0:T(8,128)(2,1)S(1)} collective-permute-done((bf16[3,4,16,256]{3,2,1,0:T(8,128)(2,1)S(1)}, bf16[3,4,16,256]{3,2,1,0:T(8,128)(2,1)S(1)}, u32[]{:S(2)}, u32[]{:S(2)}) %collective-permute-start.3) | collective-permute-done | bytes 98336 | tf_op jit(solution)/shard_map/ppermute | solution.py:251
  64.8 0.0 copy-done.1
  64.8 1.2 %shard_map.68.after_ref.near_ref = f32[4,16,256]{2,1,0:T(8,128)S(1)} custom-call(s32[2,16]{1,0:T(2,128)S(1)} %bitcast.6, bf16[16,1024]{1,0:T(8,128)(2,1)S(1)} %copy-done.4, bf16[5,4,16,256]{3,2,1,0:T(8,128)(2,1)S(1)} %collective-permute-done.got_ref.mate_ref, f32[4,16,256]{2,1,0:T(8,128)S(1)} %get-tuple-element.15.home_ref, ...), custom_call_target="tpu_custom_call" | custom-call | flops 500000000 | bytes 2500000 | tf_op jit(solution)/shard_map/pallas_call | solution.py:298
  66.0 1.7 %all-to-all-done.1.x_ref.back_ref = bf16[8,2,4,16,256]{4,3,2,1,0:T(8,128)(2,1)S(1)} async-done(((bf16[8,2,4,16,256]{4,3,2,1,0:T(8,128)(2,1)}), bf16[8,2,4,16,256]{4,3,2,1,0:T(8,128)(2,1)S(1)}, u32[]{:S(2)}, u32[]{:S(2)}) %all-to-all-start.1) | async-done | bytes 524320 | tf_op jit(solution)/shard_map/all_to_all | solution.py:318
  67.7 0.5 shard_map.69
  68.2 0.0 copy-start.2
  68.3 0.0 copy-start.3
  68.3 18.6 %all_to_all.16 = bf16[8,16,16,256]{3,2,1,0:T(8,128)(2,1)S(1)} all-to-all(bf16[8,16,16,256]{3,2,1,0:T(8,128)(2,1)S(1)} %shard_map.69), channel_id=1, replica_groups=mesh['y'=4,'zh'=8,'e'=2,'x'=4,'c'=2] {'y','e'}, dimensions={0} | all-to-all | bytes 2097152 | tf_op jit(solution)/shard_map/all_to_all | solution.py:328
  86.9 0.0 copy-done.2
  86.9 0.0 copy-done.3
  86.9 2.3 %shard_map.70 = bf16[16,1024]{1,0:T(8,128)(2,1)} custom-call(s32[2,64]{1,0:T(2,128)S(1)} %get-tuple-element.12.slot_ref, bf16[128,16,256]{2,1,0:T(8,128)(2,1)S(1)} %bitcast.4, bf16[64,32,256]{2,1,0:T(8,128)(2,1)S(1)} %copy-done.2, bf16[64,32,256]{2,1,0:T(8,128)(2,1)S(1)} %copy-done.3, f32[4,16,256]{2,1,0:T(8,128)S(1)} %shard_map.68.after_ref.near_ref, ...), custom_call_target="tpu_custom_call" | custom-call | flops 1000000000 | bytes 3500000 | tf_op jit(solution)/shard_map/pallas_call | solution.py:329
  (1 shorter events, 0.0 us)
Async XLA Ops:
  4.8 22.5 %copy-start.4 = (bf16[16,1024]{1,0:T(8,128)(2,1)S(1)}, bf16[16,1024]{1,0:T(8,128)(2,1)}, u32[]{:S(2)}) copy-start(bf16[16,1024]{1,0:T(8,128)(2,1)} %x_ref.7) | copy-start | bytes 98308
  27.2 15.4 %copy-start.5 = (s32[16,2]{0,1:T(2,128)S(1)}, s32[16,2]{0,1:T(2,128)}, u32[]{:S(2)}) copy-start(s32[16,2]{0,1:T(2,128)} %param.7) | copy-start | bytes 388
  27.2 15.4 %copy-start.6 = (s32[64,2]{0,1:T(2,128)S(1)}, s32[64,2]{0,1:T(2,128)}, u32[]{:S(2)}) copy-start(s32[64,2]{0,1:T(2,128)} %param.9) | copy-start | bytes 1540
  28.8 38.9 %all-to-all-start.1 = ((bf16[8,2,4,16,256]{4,3,2,1,0:T(8,128)(2,1)}), bf16[8,2,4,16,256]{4,3,2,1,0:T(8,128)(2,1)S(1)}, u32[]{:S(2)}, u32[]{:S(2)}) async-start(bf16[8,2,4,16,256]{4,3,2,1,0:T(8,128)(2,1)} %shard_map.66), calls=%async_computation.1 | async-start | bytes 1048576 | tf_op jit(solution)/shard_map/all_to_all | solution.py:318
  42.7 1.6 %copy-start = (bf16[16,256,256]{2,1,0:T(8,128)(2,1)S(1)}, bf16[16,256,256]{2,1,0:T(8,128)(2,1)}, u32[]{:S(2)}) copy-start(bf16[16,256,256]{2,1,0:T(8,128)(2,1)} %rest_3_.1) | copy-start | bytes 6291460
  44.2 20.5 %copy-start.1 = (bf16[16,256,256]{2,1,0:T(8,128)(2,1)S(1)}, bf16[16,256,256]{2,1,0:T(8,128)(2,1)}, u32[]{:S(2)}) copy-start(bf16[16,256,256]{2,1,0:T(8,128)(2,1)} %rest_3_.1) | copy-start | bytes 6291460
  47.0 3.3 %collective-permute-start = (bf16[5,4,16,256]{3,2,1,0:T(8,128)(2,1)S(1)}, bf16[5,4,16,256]{3,2,1,0:T(8,128)(2,1)S(1)}, u32[]{:S(2)}, u32[]{:S(2)}) collective-permute-start(bf16[5,4,16,256]{3,2,1,0:T(8,128)(2,1)S(1)} %get-tuple-element.13), channel_id=1, source_target_pairs={{0,1},{1,0},{2,3},{3,2},{4,5},{5,4},{6,7},{7,6},{8,9},{9,8},{10,11... | collective-permute-start | bytes 491528 | tf_op jit(solution)/shard_map/ppermute | solution.py:251
  50.3 8.7 %collective-permute-start.1 = (bf16[3,4,16,256]{3,2,1,0:T(8,128)(2,1)S(1)}, bf16[3,4,16,256]{3,2,1,0:T(8,128)(2,1)S(1)}, u32[]{:S(2)}, u32[]{:S(2)}) collective-permute-start(bf16[3,4,16,256]{3,2,1,0:T(8,128)(2,1)S(1)} %get-tuple-element.16), channel_id=1, source_target_pairs={{0,2},{2,4},{4,6},{6,0},{1,3},{3,5},{5,7},{7,1},{8,10},{10,12},{12... | collective-permute-start | bytes 294920 | tf_op jit(solution)/shard_map/ppermute | solution.py:251
  52.7 8.0 %collective-permute-start.2 = (bf16[3,4,16,256]{3,2,1,0:T(8,128)(2,1)S(1)}, bf16[3,4,16,256]{3,2,1,0:T(8,128)(2,1)S(1)}, u32[]{:S(2)}, u32[]{:S(2)}) collective-permute-start(bf16[3,4,16,256]{3,2,1,0:T(8,128)(2,1)S(1)} %get-tuple-element.17), channel_id=1, source_target_pairs={{0,4},{2,6},{4,0},{6,2},{1,5},{3,7},{5,1},{7,3},{8,12},{10,14},{12... | collective-permute-start | bytes 294920 | tf_op jit(solution)/shard_map/ppermute | solution.py:251
  57.1 7.7 %collective-permute-start.3 = (bf16[3,4,16,256]{3,2,1,0:T(8,128)(2,1)S(1)}, bf16[3,4,16,256]{3,2,1,0:T(8,128)(2,1)S(1)}, u32[]{:S(2)}, u32[]{:S(2)}) collective-permute-start(bf16[3,4,16,256]{3,2,1,0:T(8,128)(2,1)S(1)} %get-tuple-element.18), channel_id=1, source_target_pairs={{0,6},{2,0},{4,2},{6,4},{1,7},{3,1},{5,3},{7,5},{8,14},{10,8},{12,... | collective-permute-start | bytes 294920 | tf_op jit(solution)/shard_map/ppermute | solution.py:251
  68.2 18.7 %copy-start.2 = (bf16[64,32,256]{2,1,0:T(8,128)(2,1)S(1)}, bf16[64,32,256]{2,1,0:T(8,128)(2,1)}, u32[]{:S(2)}) copy-start(bf16[64,32,256]{2,1,0:T(8,128)(2,1)} %left_ref.1) | copy-start | bytes 3145732
  68.3 18.7 %copy-start.3 = (bf16[64,32,256]{2,1,0:T(8,128)(2,1)S(1)}, bf16[64,32,256]{2,1,0:T(8,128)(2,1)}, u32[]{:S(2)}) copy-start(bf16[64,32,256]{2,1,0:T(8,128)(2,1)} %right_ref.1) | copy-start | bytes 3145732

commit v5 on v3

--- a/solution.py
+++ b/solution.py
@@ -60,13 +60,21 @@
     return row == col
 
 
+def quotient(value, power):
+    return value >> (power.bit_length() - 1)
+
+
+def remainder(value, power):
+    return value & (power - 1)
+
+
 def slot_of(source, count):
-    owner = source // (GRP * CL)
+    owner = quotient(source, GRP * CL)
     order = count[owner]
     count[owner] = order + 1
-    y = owner // (NZH * NZL)
-    zh = (owner // NZL) % NZH
-    zl = owner % NZL
+    y = quotient(owner, NZH * NZL)
+    zh = remainder(quotient(owner, NZL), NZH)
+    zl = remainder(owner, NZL)
     peer = y * NZL + zl
     return peer, zh * CAP + order
 
@@ -97,9 +105,9 @@
             peer, within = slot_of(source, count)
             slots.append(peer * (SLOTS + 1) + within)
             table[pl.ds(peer * SLOTS + within, 1), :] = jnp.full(
-                (1, PANELS), (source % CL).astype(F32)
+                (1, PANELS), remainder(source, CL).astype(F32)
             )
-        targets = [far_ref[0, g * BATCH + i] % CL for i in range(BATCH)]
+        targets = [remainder(far_ref[0, g * BATCH + i], CL) for i in range(BATCH)]
         xt = jnp.concatenate(
             [x_ref[:, pl.ds(pl.multiple_of(t * PANELS, PANELS), PANELS)] for t in targets], axis=0
         )
@@ -121,15 +129,15 @@
     for n in range(FAR):
         peer, within = slot_of(far_ref[1, n], count)
         slot_out[0, n] = peer * SLOTS + within
-        slot_out[1, n] = far_ref[0, n] % CL
+        slot_out[1, n] = remainder(far_ref[0, n], CL)
     x = lax.axis_index("x")
     c = lax.axis_index("c")
     for w in range(CL):
         swap_out[0, w] = x_ref[:, w * PANELS:(w + 1) * PANELS]
     near_sum[...] = jnp.zeros(near_sum.shape, F32)
     for n in range(NEAR):
-        source = near_ref[1, n] % (GRP * CL)
-        start = pl.multiple_of((near_ref[0, n] % CL) * PANELS, PANELS)
+        source = remainder(near_ref[1, n], GRP * CL)
+        start = pl.multiple_of((remainder(near_ref[0, n], CL)) * PANELS, PANELS)
         near_sum[source] += dot_nn(x_ref[:, pl.ds(start, PANELS)], blocks_ref[n])
     for k in range(NX):
         at = ((x + k) % NX) * (NC * CL)
@@ -206,11 +214,11 @@
             total = total + got_refs[k - 1][2, w].astype(F32)
         out_ref[w] = total
     for n in range(NEAR):
-        source = near_ref[1, n] % (GRP * CL)
-        x_at = source // (NC * CL)
-        c_at = (source // CL) % NC
-        holder = ((x - x_at + NX) % NX) * NC + (c_at + c) % NC
-        out_ref[near_ref[0, n] % CL] += dot_nt(region[holder, source % CL], blocks_ref[n])
+        source = remainder(near_ref[1, n], GRP * CL)
+        x_at = quotient(source, NC * CL)
+        c_at = remainder(quotient(source, CL), NC)
+        holder = remainder(x - x_at + NX, NX) * NC + remainder(c_at + c, NC)
+        out_ref[remainder(near_ref[0, n], CL)] += dot_nt(region[holder, remainder(source, CL)], blocks_ref[n])
 
 
 def far_kernel(

time: 89.6 us -> 89.3 us (level)
  Pallas kernels: 13 us -> 11.7 us
  waiting for transfers between devices: 8.64 us -> 9.58 us
    pallas_call x1, Pallas kernels: 2.75 us -> 1.8 us  [on_device(): call(near_send_kernel, (shape((1 + NX, *block)), shape((NX, *block), F32)...]
    all_to_all x1, waiting for transfers between devices: 3.57 us -> 4.51 us  [on_device(): lax.all_to_all(merged, 'zh', 0, 0, axis_index_groups=[list(range(NZH))[::...]
  transfers between devices with their start and end apart: 5 -> 5, of which waited for: 4 -> 4; matrix products, arithmetic and copies ran while one was open for 0% -> 0% of each run, Pallas kernels for 4% -> 3%
where the time goes in v5:
time: 89.3 us; the launch traced here: 88.8 us
  blocking collectives  41.1 us (46%)
  starting transfers between devices  24.6 us (28%)
  Pallas kernels  11.7 us (13%)
  waiting for transfers between devices  9.58 us (11%)
  local copies, waits for them, and re-layouts  1.62 us (2%)
    all_to_all x1, blocking collectives, on_device(): lax.all_to_all(far_send.reshape(PEERS, SLOTS + 1, RHS, PANELS), ('y', 'e'...  22.4 us
    all_to_all x1, blocking collectives, on_device(): far_sources = lax.all_to_all(picked, ('y', 'e'), 0, 0, tiled=True)  18.6 us
    all_to_all x1, starting transfers between devices, on_device(): lax.all_to_all(merged, 'zh', 0, 0, axis_index_groups=[list(range(NZH))[::...  13.9 us
    ppermute x4, starting transfers between devices, shift(): lax.ppermute(array, axis, [(i, (i + by) % size) for i in range(size)])  10.8 us
    ppermute x4, waiting for transfers between devices, shift(): lax.ppermute(array, axis, [(i, (i + by) % size) for i in range(size)])  5.07 us
    all_to_all x1, waiting for transfers between devices, on_device(): lax.all_to_all(merged, 'zh', 0, 0, axis_index_groups=[list(range(NZH))[::...  4.51 us
    pallas_call x1, Pallas kernels, on_device(): call(far_send_kernel, shape((PEERS * (SLOTS + 1), RHS, PANELS)), [ANY] *...  4.34 us
    pallas_call x1, Pallas kernels, on_device(): call(far_kernel, shape(sources.shape), [SMEM] + [VMEM] * 5, VMEM, [pltpu....  2.27 us
  transfers between devices with their start and end apart: 5, of which 4 were waited for; matrix products, arithmetic and copies ran while one was open for 0% of the time, Pallas kernels for 3%

profile of v5, /device:TPU:68, one launch (start us, length us, event | category | flops | bytes accessed | tf_op | source)
XLA Modules:
  0.0 88.8 jit_solution(10201833999554220055)
XLA Ops:
  0.0 4.3 %shard_map.65 = bf16[136,16,256]{2,1,0:T(8,128)(2,1)} custom-call(s32[2,64]{1,0:T(2,128)} %bitcast.7, bf16[16,1024]{1,0:T(8,128)(2,1)} %x_ref.7, bf16[64,32,256]{2,1,0:T(8,128)(2,1)} %left_ref.1, bf16[64,32,256]{2,1,0:T(8,128)(2,1)} %right_ref.1), custom_call_target="tpu_custom_call" | custom-call | flops 1000000000 | bytes 3500000 | tf_op jit(solution)/shard_map/pallas_call | solution.py:257
  4.3 0.0 copy-start.4
  4.4 22.4 %all_to_all.15.in_ref.table_ref = bf16[8,17,16,256]{3,2,1,0:T(8,128)(2,1)S(1)} all-to-all(bf16[8,17,16,256]{3,2,1,0:T(8,128)(2,1)} %bitcast.9), channel_id=1, replica_groups=mesh['y'=4,'zh'=8,'e'=2,'x'=4,'c'=2] {'y','e'}, dimensions={0} | all-to-all | bytes 2228224 | tf_op jit(solution)/shard_map/all_to_all | solution.py:274
  26.8 0.0 copy-done.4
  26.8 0.0 copy-start.5
  26.8 0.0 copy-start.6
  26.8 1.5 %shard_map.66 = bf16[8,2,4,16,256]{4,3,2,1,0:T(8,128)(2,1)} custom-call(bf16[16,1024]{1,0:T(8,128)(2,1)S(1)} %copy-done.4, bf16[8,17,16,256]{3,2,1,0:T(8,128)(2,1)S(1)} %all_to_all.15.in_ref.table_ref), custom_call_target="tpu_custom_call" | custom-call | bytes 2000000 | tf_op jit(solution)/shard_map/pallas_call | solution.py:305
  28.4 13.9 %all-to-all-start.1 = ((bf16[8,2,4,16,256]{4,3,2,1,0:T(8,128)(2,1)}), bf16[8,2,4,16,256]{4,3,2,1,0:T(8,128)(2,1)S(1)}, u32[]{:S(2)}, u32[]{:S(2)}) async-start(bf16[8,2,4,16,256]{4,3,2,1,0:T(8,128)(2,1)} %shard_map.66), calls=%async_computation.1 | async-start | bytes 1048576 | tf_op jit(solution)/shard_map/all_to_all | solution.py:317
  42.2 0.0 copy-done.5
  42.2 0.0 copy-done.6
  42.2 0.0 copy-start
  42.2 1.6 %copy-done = bf16[16,256,256]{2,1,0:T(8,128)(2,1)S(1)} copy-done((bf16[16,256,256]{2,1,0:T(8,128)(2,1)S(1)}, bf16[16,256,256]{2,1,0:T(8,128)(2,1)}, u32[]{:S(2)}) %copy-start) | copy-done | bytes 2097176
  43.8 0.0 copy-start.1
  43.8 1.8 %shard_map.64 = (bf16[5,4,16,256]{3,2,1,0:T(8,128)(2,1)S(1)}, f32[4,4,16,256]{3,2,1,0:T(8,128)S(1)}, s32[2,64]{1,0:T(2,128)S(1)}) custom-call(s32[2,16]{1,0:T(2,128)S(1)} %bitcast.5, s32[2,64]{1,0:T(2,128)S(1)} %bitcast.8, bf16[16,1024]{1,0:T(8,128)(2,1)S(1)} %copy-done.4, bf16[16,256,256]{2,1,0:T(8,128)(2,1)S(1)} %copy-done), custom_call_target="tpu_custom_call" | custom-call | flops 1000000000 | bytes 3500000 | tf_op jit(solution)/shard_map/pallas_call | solution.py:277
  45.6 1.9 %collective-permute-start = (bf16[5,4,16,256]{3,2,1,0:T(8,128)(2,1)S(1)}, bf16[5,4,16,256]{3,2,1,0:T(8,128)(2,1)S(1)}, u32[]{:S(2)}, u32[]{:S(2)}) collective-permute-start(bf16[5,4,16,256]{3,2,1,0:T(8,128)(2,1)S(1)} %get-tuple-element.13), channel_id=1, source_target_pairs={{0,1},{1,0},{2,3},{3,2},{4,5},{5,4},{6,7},{7,6},{8,9},{9,8},{10,11... | collective-permute-start | bytes 491528 | tf_op jit(solution)/shard_map/ppermute | solution.py:250
  47.5 1.4 %collective-permute-done.got_ref.mate_ref = bf16[5,4,16,256]{3,2,1,0:T(8,128)(2,1)S(1)} collective-permute-done((bf16[5,4,16,256]{3,2,1,0:T(8,128)(2,1)S(1)}, bf16[5,4,16,256]{3,2,1,0:T(8,128)(2,1)S(1)}, u32[]{:S(2)}, u32[]{:S(2)}) %collective-permute-start) | collective-permute-done | bytes 163872 | tf_op jit(solution)/shard_map/ppermute | solution.py:250
  48.9 3.1 %collective-permute-start.1 = (bf16[3,4,16,256]{3,2,1,0:T(8,128)(2,1)S(1)}, bf16[3,4,16,256]{3,2,1,0:T(8,128)(2,1)S(1)}, u32[]{:S(2)}, u32[]{:S(2)}) collective-permute-start(bf16[3,4,16,256]{3,2,1,0:T(8,128)(2,1)S(1)} %get-tuple-element.16), channel_id=1, source_target_pairs={{0,2},{2,4},{4,6},{6,0},{1,3},{3,5},{5,7},{7,1},{8,10},{10,12},{12... | collective-permute-start | bytes 294920 | tf_op jit(solution)/shard_map/ppermute | solution.py:250
  52.1 2.7 %collective-permute-start.2 = (bf16[3,4,16,256]{3,2,1,0:T(8,128)(2,1)S(1)}, bf16[3,4,16,256]{3,2,1,0:T(8,128)(2,1)S(1)}, u32[]{:S(2)}, u32[]{:S(2)}) collective-permute-start(bf16[3,4,16,256]{3,2,1,0:T(8,128)(2,1)S(1)} %get-tuple-element.17), channel_id=1, source_target_pairs={{0,4},{2,6},{4,0},{6,2},{1,5},{3,7},{5,1},{7,3},{8,12},{10,14},{12... | collective-permute-start | bytes 294920 | tf_op jit(solution)/shard_map/ppermute | solution.py:250
  54.8 3.0 %collective-permute-start.3 = (bf16[3,4,16,256]{3,2,1,0:T(8,128)(2,1)S(1)}, bf16[3,4,16,256]{3,2,1,0:T(8,128)(2,1)S(1)}, u32[]{:S(2)}, u32[]{:S(2)}) collective-permute-start(bf16[3,4,16,256]{3,2,1,0:T(8,128)(2,1)S(1)} %get-tuple-element.18), channel_id=1, source_target_pairs={{0,6},{2,0},{4,2},{6,4},{1,7},{3,1},{5,3},{7,5},{8,14},{10,8},{12,... | collective-permute-start | bytes 294920 | tf_op jit(solution)/shard_map/ppermute | solution.py:250
  57.8 0.0 collective-permute-done.1.rest_0_
  57.8 2.2 %collective-permute-done.2.rest_1_ = bf16[3,4,16,256]{3,2,1,0:T(8,128)(2,1)S(1)} collective-permute-done((bf16[3,4,16,256]{3,2,1,0:T(8,128)(2,1)S(1)}, bf16[3,4,16,256]{3,2,1,0:T(8,128)(2,1)S(1)}, u32[]{:S(2)}, u32[]{:S(2)}) %collective-permute-start.2) | collective-permute-done | bytes 98336 | tf_op jit(solution)/shard_map/ppermute | solution.py:250
  60.1 1.5 %collective-permute-done.3.rest_2_ = bf16[3,4,16,256]{3,2,1,0:T(8,128)(2,1)S(1)} collective-permute-done((bf16[3,4,16,256]{3,2,1,0:T(8,128)(2,1)S(1)}, bf16[3,4,16,256]{3,2,1,0:T(8,128)(2,1)S(1)}, u32[]{:S(2)}, u32[]{:S(2)}) %collective-permute-start.3) | collective-permute-done | bytes 98336 | tf_op jit(solution)/shard_map/ppermute | solution.py:250
  61.6 0.0 copy-done.1
  61.6 1.2 %shard_map.68.after_ref.near_ref = f32[4,16,256]{2,1,0:T(8,128)S(1)} custom-call(s32[2,16]{1,0:T(2,128)S(1)} %bitcast.6, bf16[16,1024]{1,0:T(8,128)(2,1)S(1)} %copy-done.4, bf16[5,4,16,256]{3,2,1,0:T(8,128)(2,1)S(1)} %collective-permute-done.got_ref.mate_ref, f32[4,16,256]{2,1,0:T(8,128)S(1)} %get-tuple-element.15.home_ref, ...), custom_call_target="tpu_custom_call" | custom-call | flops 500000000 | bytes 2500000 | tf_op jit(solution)/shard_map/pallas_call | solution.py:297
  62.8 4.5 %all-to-all-done.1.x_ref.back_ref = bf16[8,2,4,16,256]{4,3,2,1,0:T(8,128)(2,1)S(1)} async-done(((bf16[8,2,4,16,256]{4,3,2,1,0:T(8,128)(2,1)}), bf16[8,2,4,16,256]{4,3,2,1,0:T(8,128)(2,1)S(1)}, u32[]{:S(2)}, u32[]{:S(2)}) %all-to-all-start.1) | async-done | bytes 524320 | tf_op jit(solution)/shard_map/all_to_all | solution.py:317
  67.3 0.5 shard_map.69
  67.8 0.0 copy-start.2
  67.8 0.0 copy-start.3
  67.8 18.6 %all_to_all.16 = bf16[8,16,16,256]{3,2,1,0:T(8,128)(2,1)S(1)} all-to-all(bf16[8,16,16,256]{3,2,1,0:T(8,128)(2,1)S(1)} %shard_map.69), channel_id=1, replica_groups=mesh['y'=4,'zh'=8,'e'=2,'x'=4,'c'=2] {'y','e'}, dimensions={0} | all-to-all | bytes 2097152 | tf_op jit(solution)/shard_map/all_to_all | solution.py:327
  86.5 0.0 copy-done.2
  86.5 0.0 copy-done.3
  86.5 2.3 %shard_map.70 = bf16[16,1024]{1,0:T(8,128)(2,1)} custom-call(s32[2,64]{1,0:T(2,128)S(1)} %get-tuple-element.12.slot_ref, bf16[128,16,256]{2,1,0:T(8,128)(2,1)S(1)} %bitcast.4, bf16[64,32,256]{2,1,0:T(8,128)(2,1)S(1)} %copy-done.2, bf16[64,32,256]{2,1,0:T(8,128)(2,1)S(1)} %copy-done.3, f32[4,16,256]{2,1,0:T(8,128)S(1)} %shard_map.68.after_ref.near_ref, ...), custom_call_target="tpu_custom_call" | custom-call | flops 1000000000 | bytes 3500000 | tf_op jit(solution)/shard_map/pallas_call | solution.py:328
  (1 shorter events, 0.0 us)
Async XLA Ops:
  4.3 22.5 %copy-start.4 = (bf16[16,1024]{1,0:T(8,128)(2,1)S(1)}, bf16[16,1024]{1,0:T(8,128)(2,1)}, u32[]{:S(2)}) copy-start(bf16[16,1024]{1,0:T(8,128)(2,1)} %x_ref.7) | copy-start | bytes 98308
  26.8 15.4 %copy-start.5 = (s32[16,2]{0,1:T(2,128)S(1)}, s32[16,2]{0,1:T(2,128)}, u32[]{:S(2)}) copy-start(s32[16,2]{0,1:T(2,128)} %param.7) | copy-start | bytes 388
  26.8 15.4 %copy-start.6 = (s32[64,2]{0,1:T(2,128)S(1)}, s32[64,2]{0,1:T(2,128)}, u32[]{:S(2)}) copy-start(s32[64,2]{0,1:T(2,128)} %param.9) | copy-start | bytes 1540
  28.4 38.9 %all-to-all-start.1 = ((bf16[8,2,4,16,256]{4,3,2,1,0:T(8,128)(2,1)}), bf16[8,2,4,16,256]{4,3,2,1,0:T(8,128)(2,1)S(1)}, u32[]{:S(2)}, u32[]{:S(2)}) async-start(bf16[8,2,4,16,256]{4,3,2,1,0:T(8,128)(2,1)} %shard_map.66), calls=%async_computation.1 | async-start | bytes 1048576 | tf_op jit(solution)/shard_map/all_to_all | solution.py:317
  42.2 1.6 %copy-start = (bf16[16,256,256]{2,1,0:T(8,128)(2,1)S(1)}, bf16[16,256,256]{2,1,0:T(8,128)(2,1)}, u32[]{:S(2)}) copy-start(bf16[16,256,256]{2,1,0:T(8,128)(2,1)} %rest_3_.1) | copy-start | bytes 6291460
  43.8 17.7 %copy-start.1 = (bf16[16,256,256]{2,1,0:T(8,128)(2,1)S(1)}, bf16[16,256,256]{2,1,0:T(8,128)(2,1)}, u32[]{:S(2)}) copy-start(bf16[16,256,256]{2,1,0:T(8,128)(2,1)} %rest_3_.1) | copy-start | bytes 6291460
  45.6 3.3 %collective-permute-start = (bf16[5,4,16,256]{3,2,1,0:T(8,128)(2,1)S(1)}, bf16[5,4,16,256]{3,2,1,0:T(8,128)(2,1)S(1)}, u32[]{:S(2)}, u32[]{:S(2)}) collective-permute-start(bf16[5,4,16,256]{3,2,1,0:T(8,128)(2,1)S(1)} %get-tuple-element.13), channel_id=1, source_target_pairs={{0,1},{1,0},{2,3},{3,2},{4,5},{5,4},{6,7},{7,6},{8,9},{9,8},{10,11... | collective-permute-start | bytes 491528 | tf_op jit(solution)/shard_map/ppermute | solution.py:250
  48.9 8.9 %collective-permute-start.1 = (bf16[3,4,16,256]{3,2,1,0:T(8,128)(2,1)S(1)}, bf16[3,4,16,256]{3,2,1,0:T(8,128)(2,1)S(1)}, u32[]{:S(2)}, u32[]{:S(2)}) collective-permute-start(bf16[3,4,16,256]{3,2,1,0:T(8,128)(2,1)S(1)} %get-tuple-element.16), channel_id=1, source_target_pairs={{0,2},{2,4},{4,6},{6,0},{1,3},{3,5},{5,7},{7,1},{8,10},{10,12},{12... | collective-permute-start | bytes 294920 | tf_op jit(solution)/shard_map/ppermute | solution.py:250
  52.1 8.0 %collective-permute-start.2 = (bf16[3,4,16,256]{3,2,1,0:T(8,128)(2,1)S(1)}, bf16[3,4,16,256]{3,2,1,0:T(8,128)(2,1)S(1)}, u32[]{:S(2)}, u32[]{:S(2)}) collective-permute-start(bf16[3,4,16,256]{3,2,1,0:T(8,128)(2,1)S(1)} %get-tuple-element.17), channel_id=1, source_target_pairs={{0,4},{2,6},{4,0},{6,2},{1,5},{3,7},{5,1},{7,3},{8,12},{10,14},{12... | collective-permute-start | bytes 294920 | tf_op jit(solution)/shard_map/ppermute | solution.py:250
  54.8 6.8 %collective-permute-start.3 = (bf16[3,4,16,256]{3,2,1,0:T(8,128)(2,1)S(1)}, bf16[3,4,16,256]{3,2,1,0:T(8,128)(2,1)S(1)}, u32[]{:S(2)}, u32[]{:S(2)}) collective-permute-start(bf16[3,4,16,256]{3,2,1,0:T(8,128)(2,1)S(1)} %get-tuple-element.18), channel_id=1, source_target_pairs={{0,6},{2,0},{4,2},{6,4},{1,7},{3,1},{5,3},{7,5},{8,14},{10,8},{12,... | collective-permute-start | bytes 294920 | tf_op jit(solution)/shard_map/ppermute | solution.py:250
  67.8 18.7 %copy-start.2 = (bf16[64,32,256]{2,1,0:T(8,128)(2,1)S(1)}, bf16[64,32,256]{2,1,0:T(8,128)(2,1)}, u32[]{:S(2)}) copy-start(bf16[64,32,256]{2,1,0:T(8,128)(2,1)} %left_ref.1) | copy-start | bytes 3145732
  67.8 18.7 %copy-start.3 = (bf16[64,32,256]{2,1,0:T(8,128)(2,1)S(1)}, bf16[64,32,256]{2,1,0:T(8,128)(2,1)}, u32[]{:S(2)}) copy-start(bf16[64,32,256]{2,1,0:T(8,128)(2,1)} %right_ref.1) | copy-start | bytes 3145732
